TPU v7x, 128 devices: a whole 4x4x4 slice. The times are simulated.
128 devices in a mesh: dp: 8 (over z, y_hi), tensor: 16 (over y_lo, x, core).
Axes of the slice: x: 4, y: 4 (y_hi: 2, y_lo: 2; y = y_hi * 2 + y_lo), z: 4, core: 2. Of those that a mesh axis runs over, the one named last changes fastest.
Arguments:
- inputs: bfloat16 [1024, 7424], P(('dp', 'tensor')), may hold values from -6 to 6
- grad_out: bfloat16 [1024, 7424], P(('dp', 'tensor')), may hold values from -6 to 6
- w_in: bfloat16 [7424, 29696], P('tensor', 'dp'), may hold values from -0.0625 to 0.0625
- w_out: bfloat16 [29696, 7424], P('dp', 'tensor'), may hold values from -0.03125 to 0.03125
Outputs:
- grad_x: bfloat16 [1024, 7424], P(('dp', 'tensor'))
- grad_w1: float32 [7424, 29696], P('tensor', 'dp')
- grad_w2: float32 [29696, 7424], P('dp', 'tensor')
All inputs are finite; a program needn't handle non-finite values.
Results may differ from a plain program's by a relative error of at most 0.028.
Values may be sent and summed in bfloat16 or wider, within the bound.
No kernel may reach another device: no remote copies, remote signals or barrier semaphores. Data moves between devices by JAX's collectives and lax.ppermute only.
A program may use at most 128 MiB of HBM per device.

v0:
```python
import functools
import math

import jax
import jax.numpy as jnp
from jax import lax
from jax.experimental import pallas as pl
from jax.experimental.pallas import tpu as pltpu
from jax.sharding import Mesh
from jax.sharding import PartitionSpec as P

inv_root_two = 0.7071067811865476
inv_root_two_pi = 0.3989422804014327
AXES = ("z", "yh", "y", "x", "core")
TILE = 128
SPLIT_DH = 17
WIDTH = 4
WIDE = 8
bf16, f32 = jnp.bfloat16, jnp.float32


def gelu_parts(hidden):
    normal_cdf = 0.5 * (1.0 + lax.erf(hidden * inv_root_two))
    return (
        hidden * normal_cdf,
        normal_cdf + hidden * jnp.exp(-0.5 * hidden * hidden) * inv_root_two_pi,
    )


def ring(axis, step):
    return lambda v: lax.ppermute(v, axis, [(i, (i + step) % 4) for i in range(4)])


def swap(axis):
    return lambda v: lax.ppermute(v, axis, [(0, 1), (1, 0)])


def x_links():
    return ring("x", 1), ring("x", -1), ring("x", 2), swap("y")


def padded(shape, dtype):
    *lead, rows, cols = shape
    return math.prod(lead) * -(-rows // 16) * 16 * -(-cols // TILE) * TILE * jnp.dtype(dtype).itemsize


def call(body, outs, operands, scratch=(), smem=0, after=(), sems=(), token=False, hbm=0, hbm_out=False, light=False):
    held = [padded(v.shape, v.dtype) for v in operands[smem : len(operands) - hbm]]
    held += [padded(s, d) for s, d in (*(() if hbm_out else outs), *scratch)]
    n, m, k = len(operands), len(after), len(outs)
    outs = [*outs, ((8, TILE), f32)] if token else outs

    def run(*refs):
        given, made = refs[:n], refs[n + m :]
        body(*given, *made[:k], *made[len(outs) :])
        if token:
            made[k][...] = jnp.zeros((8, TILE), f32)

    spaces = [pltpu.SMEM] * smem + [pltpu.VMEM] * (n - smem - hbm) + [pltpu.HBM] * hbm + [pl.ANY] * m
    return pl.pallas_call(
        run,
        out_shape=[jax.ShapeDtypeStruct(s, d) for s, d in outs],
        in_specs=[pl.BlockSpec(memory_space=space) for space in spaces],
        out_specs=[pl.BlockSpec(memory_space=pltpu.HBM if hbm_out and i < k else pltpu.VMEM) for i in range(len(outs))],
        scratch_shapes=[pltpu.VMEM(s, d) for s, d in scratch] + [pltpu.SemaphoreType.DMA(v) for v in sems],
        compiler_params=pltpu.CompilerParams(vmem_limit_bytes=sum(held) + 4 * 2**20),
        cost_estimate=pl.CostEstimate(flops=0, bytes_accessed=0 if light else sum(held), transcendentals=0),
    )(*operands, *after)


def dot(left, right, dims):
    return lax.dot_general(left, right, (dims, ((), ())), preferred_element_type=f32)


def groups(count, size, step):
    whole = count // size
    if whole:
        pl.loop(0, whole)(lambda i: step(size * i, size))
    if count % size:
        step(size * whole, count % size)


def held_until(arrays, after):
    n = len(arrays)
    return pl.pallas_call(
        lambda *refs: None,
        out_shape=[jax.ShapeDtypeStruct(v.shape, v.dtype) for v in arrays],
        in_specs=[pl.BlockSpec(memory_space=pl.ANY)] * (n + len(after)),
        out_specs=[pl.BlockSpec(memory_space=pl.ANY)] * n,
        input_output_aliases={i: i for i in range(n)},
    )(*arrays, *after)


class Streamed:
    def __init__(self, sources, target, sems, width):
        self.feats, self.sems, self.width, self.target = sources[0].shape[0], sems, width, target
        self.sources, self.room = sources, target.shape[0] // 2
        self.count = sources[0].shape[1] // TILE
        groups(self.count, width, self.start)
        for i in range(2):
            rest = slice(i * self.room + self.feats, (i + 1) * self.room)
            target[rest, :] = jnp.zeros((self.room - self.feats, target.shape[1]), bf16)

    def copies(self, tile, count):
        cols = columns(tile, count)
        return [
            pltpu.make_async_copy(
                ref.at[:, cols],
                self.target.at[i * self.room : i * self.room + self.feats, cols],
                self.sems.at[i, tile // self.width],
            )
            for i, ref in enumerate(self.sources)
        ]

    def start(self, tile, count):
        for c in self.copies(tile, count):
            c.start()

    def wait(self, tile, count):
        for c in self.copies(tile, count):
            c.wait()


def roomy(feats):
    return -(-feats // 256) * 256


def columns(tile, count):
    return pl.ds(tile * TILE if isinstance(tile, int) else pl.multiple_of(tile * TILE, TILE), count * TILE)


def add(*terms):
    total = terms[0].astype(f32)
    for term in terms[1:]:
        total = total + term.astype(f32)
    return total


def spread_body(core, x, g, out):
    feats = out.shape[-1]
    first = core[0] == 0
    for i, ref in enumerate((g, x)):
        v = ref[...].astype(f32)
        for chip in range(8):
            even, odd = (v[:, (2 * chip + c) * feats : (2 * chip + c + 1) * feats] for c in range(2))
            own = jnp.where(first, even, odd).astype(bf16)
            sib = jnp.where(first, odd, even).astype(bf16)
            for group in range(8):
                out[8 * group + chip, 2 * i] = own
                out[8 * group + chip, 2 * i + 1] = sib


def exchange(v):
    return lax.all_to_all(v, ("z", "yh", "y", "x"), split_axis=0, concat_axis=0, tiled=True)


def product_body(ring_first, order, *refs):
    got, *sources, own, sib = refs[:5]
    *outs, left, weight, sems = refs[5:]
    weights = Streamed(sources, weight, sems, WIDTH)
    feats, room = own.shape[1], left.shape[1] // 2
    rows = own.shape[0] // 8
    left[...] = jnp.zeros_like(left)
    for k in range(8):
        at = slice(k * rows, (k + 1) * rows)
        for half, ref in enumerate((own, sib)):
            v = got[pl.ds(order[k] * 8, 8), half + 2 * ring_first].astype(f32).reshape(rows, feats).astype(bf16)
            ref[at, :] = v
            left[at, half * room : half * room + feats] = v

    def multiply(tile, count):
        cols = columns(tile, count)
        weights.wait(tile, count)
        total = dot(left[...], weight[:, cols], ((1,), (0,))).astype(bf16)
        total = total.reshape(8, rows, count * TILE)
        for j in range(count):
            part = total[:, :, j * TILE : (j + 1) * TILE]
            if ring_first:
                for k, ref in enumerate(outs):
                    ref[tile + j] = part[k]
            else:
                for dy, ref in enumerate(outs):
                    ref[tile + j] = part[4 * dy : 4 * dy + 4]

    groups(outs[0].shape[0], WIDTH, multiply)


def product(order, got, w_own, w_sib, ring_first, after=()):
    rows, feats = 8 * got.shape[2], got.shape[3]
    nt = w_own.shape[1] // TILE
    outs = [((nt, rows, TILE), bf16)] * 8 if ring_first else [((nt, 4, rows, TILE), bf16)] * 2
    return call(
        functools.partial(product_body, ring_first),
        [((8 * rows, feats), bf16)] * 2 + outs,
        [order, got, w_own, w_sib],
        [
            ((8 * rows, 2 * roomy(feats)), bf16),
            ((2 * roomy(feats), nt * TILE), bf16),
        ],
        smem=1,
        after=after,
        hbm=2,
        sems=((2, -(-nt // WIDTH)),),
    )


def tiles(count, step):
    pl.loop(0, count)(step)


def ring_forward_body(up_own, down_own, r, l, x, g, up, down, both):
    def step(t):
        up[t] = add(up_own[t], r[t]).astype(bf16)
        down[t] = add(down_own[t], l[t]).astype(bf16)

    tiles(up.shape[0], step)
    feats, room = x.shape[1], both.shape[1] // 2
    both[:, :feats] = x[...]
    both[:, room : room + feats] = g[...]


def ring_sum_body(keep, keep_across, l_near, r_near, r_far, l_far, kept, sent):
    def step(t):
        kept[t] = add(keep[t], l_near[t], r_far[t])
        sent[t] = add(keep_across[t], r_near[t], l_far[t]).astype(bf16)

    tiles(keep.shape[0], step)


def across_sum_body(keep, y, kept, up, far, down):
    def step(t):
        total = add(keep[t], y[t])
        kept[t] = total[0]
        for dx, ref in ((1, up), (2, far), (3, down)):
            ref[t] = total[dx].astype(bf16)

    tiles(keep.shape[0], step)


def act_body(kept, y, act, slope):
    def step(t):
        a, s = gelu_parts(add(kept[t], y[t]))
        act[t] = a.astype(bf16)
        slope[t] = s

    tiles(act.shape[0], step)


def slope_body(kept, r, l, x, slope, out):
    def step(t):
        out[t] = (add(kept[t], r[t], l[t], x[t]) * slope[t]).astype(bf16)

    tiles(out.shape[0], step)


def gather_first(v):
    up, down, far, over = x_links()
    return v, over(v), up(v), down(v), far(v)


def pack_body(y, r, l, x, a, a_across, to_ring, to_over, pair):
    na = to_ring.shape[0]
    to_ring[...] = y[:na]
    for k, ref in enumerate((l, x, r)):
        to_over[:, k] = ref[na:]
    pair[:, 0] = a[...]
    pair[:, 1] = a_across[...]


def gather_second(state, na, a, a_across, after):
    up, down, far, over = x_links()
    nt, rows, _ = state[0].shape
    to_ring, to_over, pair = call(
        pack_body,
        [((na, rows, TILE), bf16), ((nt - na, 3, rows, TILE), bf16), ((nt, 2, rows, TILE), bf16)],
        (*state[1:], a, a_across),
        after=after,
    )
    return (*state, over(to_over), up(to_ring), down(to_ring), far(to_ring)), pair


def whole_body(v, y, r, l, x, y2, r2, l2, x2, out):
    na = r2.shape[0]
    for k, ref in enumerate((v, l, x, r, y)):
        out[:, k] = ref[...]
    for k, ref in enumerate((l2, x2, r2)):
        out[:na, 5 + k] = ref[...]
    out[na:, 5:] = y2[...]


def gather_end(state):
    nt, rows, _ = state[0].shape
    whole = call(whole_body, [((nt, 8, rows, TILE), bf16)], state)[0]
    return whole, swap("core")(whole)


def forward_body(pair, r, l, up, down, near):
    up[...] = r[:, 0]
    down[...] = l[:, 1]
    for k, ref in enumerate((pair, l, r)):
        near[:, 2 * k : 2 * k + 2] = ref[...]


def gather_ring(pair, after):
    up, down, _, _ = x_links()
    nt, _, rows, _ = pair.shape
    r, l = up(pair), down(pair)
    to_up, to_down, near, token = call(
        forward_body,
        [((nt, rows, TILE), bf16)] * 2 + [((nt, 6, rows, TILE), bf16)],
        (pair, r, l),
        after=after,
        token=True,
    )
    return near, (up(to_up), down(to_down)), token


def token_rows(pieces, tile, count):
    wide = [pieces[0][tile + j] for j in range(count)]
    return jnp.concatenate([v.reshape(v.shape[0] * v.shape[1], TILE) for v in wide], axis=1)


def input_grad_body(order, whole, w_own, w_sib, out, total, weight, sems):
    weights = Streamed((w_own, w_sib), weight, sems, WIDE)
    nt, rows = whole.shape[0], whole.shape[2]
    (tokens, feats), room = out.shape[2:], weight.shape[0] // 2
    total[...] = jnp.zeros_like(total)

    def multiply(tile, count):
        cols = columns(tile, count)
        left = token_rows([whole], tile, count)
        weights.wait(tile, count)
        total[...] += dot(left, weight[:, cols], ((1,), (1,)))

    groups(nt, WIDE, multiply)
    for k in range(8):
        for half in range(2):
            v = total[k * rows : (k + 1) * rows, half * room : half * room + feats]
            out[pl.ds(order[k] * 8, 8), half] = v.reshape(8, tokens, feats).astype(bf16)


def pair_rows(pieces, tile, count):
    near, x_near, x_far = pieces
    wide = []
    for j in range(count):
        t = tile + j
        parts = [near[t, 0], near[t, 2], x_near[t], near[t, 4], near[t, 1], near[t, 3], x_far[t], near[t, 5]]
        wide.append(jnp.concatenate(parts, axis=0))
    return jnp.concatenate(wide, axis=1)


def transposed_body(x_own, g_own, sibs, x, g):
    (half, feats), room = x_own.shape, sibs.shape[1] // 2
    for i, (own, out) in enumerate(((x_own, x), (g_own, g))):
        out[:, :half] = own[...].T
        out[:, half:] = sibs[:, i * room : i * room + feats].T


def weight_grad_body(factor, width, rows_of, turned, *refs):
    n = (len(refs) - 4) // 2
    sources, out, right, (held, sems, in_sems) = refs[:n], refs[n], refs[n + 1 : 2 * n + 1], refs[2 * n + 1 :]
    own, sib = right[: n // 2], right[n // 2 :]
    nt = own[0].shape[0]

    def fetch(tile, count):
        part = pl.ds(tile, count)
        return [
            pltpu.make_async_copy(a.at[part], b.at[part], in_sems.at[i, tile // width])
            for i, (a, b) in enumerate(zip(sources, right))
        ]

    def start(tile, count):
        for c in fetch(tile, count):
            c.start()

    def copy(tile, count):
        cols = columns(tile, count)
        return pltpu.make_async_copy(held.at[:, cols], out.at[:, cols], sems.at[tile // width])

    def multiply(tile, count):
        for c in fetch(tile, count):
            c.wait()
        both = jnp.concatenate([rows_of(own, tile, count), rows_of(sib, tile, count)], axis=0)
        held[:, columns(tile, count)] = dot(turned[...], both, ((1,), (0,))) * factor
        copy(tile, count).start()

    groups(nt, width, start)
    groups(nt, width, multiply)
    groups(nt, width, lambda tile, count: copy(tile, count).wait())


def weight_grad(turned, own, sib, rows_of, after):
    nt, (feats, tokens) = own[0].shape[0], turned.shape
    factor = 1.0 / math.sqrt(tokens)
    shape = (feats, nt * TILE)
    right = (*own, *sib)
    steps = -(-nt // WIDTH)
    return call(
        functools.partial(weight_grad_body, factor, WIDTH, rows_of),
        [(shape, f32)],
        (turned, *right),
        [(v.shape, bf16) for v in right] + [(shape, f32)],
        hbm=len(right),
        sems=((steps,), (len(right), steps)),
        hbm_out=True,
        after=after,
        token=True,
        light=True,
    )


def join_body(core, got, out):
    first = core[0] == 0
    wide = []
    for chip in range(8):
        own, sib = (add(*(got[8 * group + chip, half] for group in range(8))) for half in range(2))
        wide += [jnp.where(first, own, sib), jnp.where(first, sib, own)]
    out[...] = jnp.concatenate(wide, axis=1).astype(bf16)


def per_device(inputs, grad_out, w_in, w_out):
    yi, xi, core = lax.axis_index("y"), lax.axis_index("x"), lax.axis_index("core")
    core = core.astype(jnp.int32).reshape(1)
    tokens, width = inputs.shape
    feats = w_in.shape[0]
    nt = w_in.shape[1] // TILE
    rows = 8 * tokens
    cc = swap("core")
    w_out = w_out.T
    w_in_sib, w_out_sib = cc(w_in), cc(w_out)

    order = jnp.stack(
        [((yi + dy) % 2) * 4 + (xi + dx) % 4 for dy in range(2) for dx in range(4)]
    ).astype(jnp.int32)
    both = call(
        spread_body, [((64, 4, tokens, feats), bf16)], (core, inputs, grad_out), smem=1
    )[0]
    both = exchange(both)

    up, down, far, over = x_links()
    g_own, g_sib, keep_g, to_over = product(order, both, w_out, w_out_sib, False)
    got_g = over(to_over)
    x_own, x_sib, *parts = product(order, both, w_in, w_in_sib, True, (keep_g,))
    r, l = up(parts[2]), down(parts[6])
    l_near, r_near = down(parts[3]), up(parts[5])
    one = (nt, rows, TILE)
    to_up, to_down, sibs = call(
        ring_forward_body,
        [(one, bf16)] * 2 + [((8 * rows, 2 * roomy(feats)), bf16)],
        (parts[1], parts[7], r, l, x_sib, g_sib),
    )
    r_far, l_far = up(to_up), down(to_down)
    kept_g, to_up, to_far, to_down = call(
        across_sum_body, [(one, f32)] + [(one, bf16)] * 3, (keep_g, got_g)
    )
    got_g = up(to_up), down(to_down), far(to_far)
    swapped = cc(sibs)
    kept, sent = call(
        ring_sum_body,
        [(one, f32), (one, bf16)],
        (parts[0], parts[4], l_near, r_near, r_far, l_far),
        after=(kept_g,),
    )
    act, slope = call(act_body, [(one, bf16), (one, f32)], (kept, over(sent)))
    act_across = over(act)
    dh = call(slope_body, [(one, bf16)], (kept_g, *got_g, slope), after=(act_across, swapped))[0]
    x_turned, g_turned = call(
        transposed_body, [((feats, 16 * rows), bf16)] * 2, (x_own, g_own, swapped)
    )
    state_d, act_pair = gather_second(
        gather_first(dh), SPLIT_DH, act, act_across, (x_turned, g_turned)
    )
    dh_own, dh_sib = gather_end(state_d)

    gx, token = call(
        input_grad_body,
        [((64, 2, tokens, feats), bf16)],
        (order, dh_own, w_in, w_in_sib),
        [((8 * rows, 2 * roomy(feats)), f32), ((2 * roomy(feats), nt * TILE), bf16)],
        smem=1,
        token=True,
        hbm=2,
        sems=((2, -(-nt // WIDE)),),
    )
    near, far, token_act = gather_ring(act_pair, (token,))
    gx = exchange(*held_until([gx], (token_act,)))
    sum_w1, token = weight_grad(x_turned, [dh_own], [dh_sib], token_rows, (token,))
    act_own = near, *far
    sum_w2, token = weight_grad(g_turned, act_own, [cc(v) for v in act_own], pair_rows, (token,))
    grad_x = call(
        join_body, [((tokens, width), bf16)], (core, gx), smem=1, after=(token,)
    )[0]
    return grad_x, sum_w1, sum_w2.T


def solution(mesh):
    inner = Mesh(mesh.devices.reshape(4, 2, 2, 4, 2), AXES)
    dp, tensor = ("z", "yh"), ("y", "x", "core")
    placed = (P(dp + tensor, None), P(dp + tensor, None), P(tensor, dp), P(dp, tensor))
    return jax.shard_map(
        per_device,
        mesh=inner,
        in_specs=placed,
        out_specs=(P(dp + tensor, None), P(tensor, dp), P(dp, tensor)),
        check_vma=False,
    )
```

profile of v0, /device:TPU:1, one launch (start us, length us, event | category | flops | bytes accessed | tf_op | source)
XLA Modules:
  0.0 221.2 jit_solution(10586925422268421272)
XLA Ops:
  0.6 1.5 collective-permute-start
  2.2 0.9 copy-done.4
  3.1 0.9 copy-done.5
  4.0 0.6 shard_map.67
  4.6 1.3 copy-done.1
  5.9 11.2 %all-to-all-start = ((bf16[64,4,8,464]{3,2,1,0:T(8,128)(2,1)}), bf16[64,4,8,464]{3,2,1,0:T(8,128)(2,1)S(1)}, u32[]{:S(2)}, u32[]{:S(2)}) async-start(bf16[64,4,8,464]{3,2,1,0:T(8,128)(2,1)} %copy-done.1), calls=%async_computation | async-start | bytes 4194304 | tf_op jit(solution)/shard_map/all_to_all | solution.py:154
  17.3 28.7 %all-to-all-done.refs_1_ = bf16[64,4,8,464]{3,2,1,0:T(8,128)(2,1)S(1)} async-done(((bf16[64,4,8,464]{3,2,1,0:T(8,128)(2,1)}), bf16[64,4,8,464]{3,2,1,0:T(8,128)(2,1)S(1)}, u32[]{:S(2)}, u32[]{:S(2)}) %all-to-all-start) | async-done | bytes 1900576 | tf_op jit(solution)/shard_map/all_to_all | solution.py:154
  46.0 2.1 copy-done.3
  48.2 7.2 %shard_map.68 = (bf16[512,464]{1,0:T(8,128)(2,1)S(1)}, bf16[512,464]{1,0:T(8,128)(2,1)S(1)}, bf16[29,4,64,128]{3,2,1,0:T(8,128)(2,1)S(1)}, bf16[29,4,64,128]{3,2,1,0:T(8,128)(2,1)S(1)}) custom-call(s32[8]{0:T(128)S(1)} %stack.35.refs_0_, bf16[64,4,8,464]{3,2,1,0:T(8,128)(2,1)S(1)} %all-to-all-done.refs_1_, bf16[464,3712]{1,0:T(8,128)(2,1)S(1)} %bitcast.12, ...), custom_call_target="tpu_custom_call" | custom-call | bytes 17694720 | tf_op jit(solution)/shard_map/pallas_call | solution.py:60
  55.4 0.4 collective-permute-start.1
  55.8 7.2 %shard_map.70 = (bf16[512,464]{1,0:T(8,128)(2,1)S(1)}, bf16[512,464]{1,0:T(8,128)(2,1)S(1)}, bf16[29,64,128]{2,1,0:T(8,128)(2,1)S(1)}, bf16[29,64,128]{2,1,0:T(8...) custom-call(s32[8]{0:T(128)S(1)} %stack.35.refs_0_, ...), custom_call_target="tpu_custom_call" | custom-call | bytes 17694720 | tf_op jit(solution)/shard_map/pallas_call | solution.py:60
  63.0 0.2 collective-permute-start.8
  63.2 2.6 %collective-permute-start.9 = (bf16[29,64,128]{2,1,0:T(8,128)(2,1)S(1)}, bf16[29,64,128]{2,1,0:T(8,128)(2,1)S(1)}, u32[]{:S(2)}, u32[]{:S(2)}) collective-permute-start(bf16[29,64,128]{2,1,0:T(8,128)(2,1)S(1)} %get-tuple-element.56), channel_id=1, source_target_pairs={{0,6},{2,0},{4,2},{6,4},{1,7},{3,1},{5,3},{7,5},{8,14},{10,8},{12,... | collective-permute-start | bytes 1425416 | tf_op jit(solution)/shard_map/ppermute | solution.py:31
  65.7 1.4 collective-permute-start.7
  67.2 7.1 %collective-permute-done.8.refs_2_ = bf16[29,64,128]{2,1,0:T(8,128)(2,1)S(1)} collective-permute-done((bf16[29,64,128]{2,1,0:T(8,128)(2,1)S(1)}, bf16[29,64,128]{2,1,0:T(8,128)(2,1)S(1)}, u32[]{:S(2)}, u32[]{:S(2)}) %collective-permute-start.8) | collective-permute-done | bytes 475168 | tf_op jit(solution)/shard_map/ppermute | solution.py:31
  74.3 0.4 shard_map.71
  74.7 0.3 collective-permute-start.10
  75.0 2.4 %collective-permute-start.11 = (bf16[29,64,128]{2,1,0:T(8,128)(2,1)S(1)}, bf16[29,64,128]{2,1,0:T(8,128)(2,1)S(1)}, u32[]{:S(2)}, u32[]{:S(2)}) collective-permute-start(bf16[29,64,128]{2,1,0:T(8,128)(2,1)S(1)} %get-tuple-element.60), channel_id=1, source_target_pairs={{0,6},{2,0},{4,2},{6,4},{1,7},{3,1},{5,3},{7,5},{8,14},{10,8},{12,... | collective-permute-start | bytes 1425416 | tf_op jit(solution)/shard_map/ppermute | solution.py:31
  77.4 18.8 %collective-permute-done.1.refs_1_ = bf16[29,4,64,128]{3,2,1,0:T(8,128)(2,1)S(1)} collective-permute-done((bf16[29,4,64,128]{3,2,1,0:T(8,128)(2,1)S(1)}, bf16[29,4,64,128]{3,2,1,0:T(8,128)(2,1)S(1)}, u32[]{:S(2)}, u32[]{:S(2)}) %collective-permute-start.1) | collective-permute-done | bytes 1900576 | tf_op jit(solution)/shard_map/ppermute | solution.py:35
  96.2 3.1 %collective-permute-start.14 = (bf16[512,1024]{1,0:T(8,128)(2,1)S(1)}, bf16[512,1024]{1,0:T(8,128)(2,1)S(1)}, u32[]{:S(2)}, u32[]{:S(2)}) collective-permute-start(bf16[512,1024]{1,0:T(8,128)(2,1)S(1)} %get-tuple-element.65), channel_id=1, source_target_pairs={{0,1},{1,0},{2,3},{3,2},{4,5},{5,4},{6,7},{7,6},{8,9},{9,8},{10,11... | collective-permute-start | bytes 3145736 | tf_op jit(solution)/shard_map/ppermute | solution.py:35
  99.3 0.5 shard_map.69
  99.9 0.5 shard_map.72
  100.3 0.4 collective-permute-start.12
  100.8 2.6 %collective-permute-start.3 = (bf16[29,64,128]{2,1,0:T(8,128)(2,1)S(1)}, bf16[29,64,128]{2,1,0:T(8,128)(2,1)S(1)}, u32[]{:S(2)}, u32[]{:S(2)}) collective-permute-start(bf16[29,64,128]{2,1,0:T(8,128)(2,1)S(1)} %get-tuple-element.47), channel_id=1, source_target_pairs={{0,6},{2,0},{4,2},{6,4},{1,7},{3,1},{5,3},{7,5},{8,14},{10,8},{12,... | collective-permute-start | bytes 1425416 | tf_op jit(solution)/shard_map/ppermute | solution.py:31
  103.4 0.2 collective-permute-start.4
  103.6 9.3 %collective-permute-done.12.refs_1_ = bf16[29,64,128]{2,1,0:T(8,128)(2,1)S(1)} collective-permute-done((bf16[29,64,128]{2,1,0:T(8,128)(2,1)S(1)}, bf16[29,64,128]{2,1,0:T(8,128)(2,1)S(1)}, u32[]{:S(2)}, u32[]{:S(2)}) %collective-permute-start.12) | collective-permute-done | bytes 475168 | tf_op jit(solution)/shard_map/ppermute | solution.py:35
  112.9 0.7 shard_map.73
  113.6 0.4 collective-permute-start.13
  114.0 10.3 %collective-permute-done.2.refs_1_ = bf16[29,64,128]{2,1,0:T(8,128)(2,1)S(1)} collective-permute-done((bf16[29,64,128]{2,1,0:T(8,128)(2,1)S(1)}, bf16[29,64,128]{2,1,0:T(8,128)(2,1)S(1)}, u32[]{:S(2)}, u32[]{:S(2)}) %collective-permute-start.2) | collective-permute-done | bytes 475168 | tf_op jit(solution)/shard_map/ppermute | solution.py:31
  124.3 1.0 collective-permute-done.13.refs_5_
  125.3 0.4 shard_map.74.refs_0_
  125.7 0.4 collective-permute-start.15
  126.1 0.5 collective-permute-start.16
  126.5 2.2 %collective-permute-start.17 = (bf16[29,64,128]{2,1,0:T(8,128)(2,1)S(1)}, bf16[29,64,128]{2,1,0:T(8,128)(2,1)S(1)}, u32[]{:S(2)}, u32[]{:S(2)}) collective-permute-start(bf16[29,64,128]{2,1,0:T(8,128)(2,1)S(1)} %shard_map.74.refs_0_), channel_id=1, source_target_pairs={{0,6},{2,0},{4,2},{6,4},{1,7},{3,1},{5,3},{7,5},{8,14},{10,8},{12,... | collective-permute-start | bytes 1425416 | tf_op jit(solution)/shard_map/ppermute | solution.py:31
  128.8 0.7 collective-permute-start.18
  129.5 0.6 shard_map.75
  130.1 6.3 %collective-permute-done.15.refs_0_.refs_1_ = bf16[29,64,128]{2,1,0:T(8,128)(2,1)S(1)} collective-permute-done((bf16[29,64,128]{2,1,0:T(8,128)(2,1)S(1)}, bf16[29,64,128]{2,1,0:T(8,128)(2,1)S(1)}, u32[]{:S(2)}, u32[]{:S(2)}) %collective-permute-start.15) | collective-permute-done | bytes 475168 | tf_op jit(solution)/shard_map/ppermute | solution.py:35
  136.5 1.2 collective-permute-done.16.refs_1_.refs_2_
  137.7 11.2 %collective-permute-done.18.refs_3_.refs_4_ = bf16[29,64,128]{2,1,0:T(8,128)(2,1)S(1)} collective-permute-done((bf16[29,64,128]{2,1,0:T(8,128)(2,1)S(1)}, bf16[29,64,128]{2,1,0:T(8,128)(2,1)S(1)}, u32[]{:S(2)}, u32[]{:S(2)}) %collective-permute-start.18) | collective-permute-done | bytes 475168 | tf_op jit(solution)/shard_map/ppermute | solution.py:31
  149.0 0.4 collective-permute-start.19
  149.4 0.5 collective-permute-start.20
  150.0 2.1 collective-permute-start.21
  152.1 0.6 collective-permute-start.23
  152.7 3.4 %collective-permute-done.20.refs_6_ = bf16[17,64,128]{2,1,0:T(8,128)(2,1)S(1)} collective-permute-done((bf16[17,64,128]{2,1,0:T(8,128)(2,1)S(1)}, bf16[17,64,128]{2,1,0:T(8,128)(2,1)S(1)}, u32[]{:S(2)}, u32[]{:S(2)}) %collective-permute-start.20) | collective-permute-done | bytes 278560 | tf_op jit(solution)/shard_map/ppermute | solution.py:31
  156.0 2.0 collective-permute-done.21.refs_7_
  158.0 2.3 %collective-permute-done.22.refs_8_ = bf16[17,64,128]{2,1,0:T(8,128)(2,1)S(1)} collective-permute-done((bf16[17,64,128]{2,1,0:T(8,128)(2,1)S(1)}, bf16[17,64,128]{2,1,0:T(8,128)(2,1)S(1)}, u32[]{:S(2)}, u32[]{:S(2)}) %collective-permute-start.22) | collective-permute-done | bytes 278560 | tf_op jit(solution)/shard_map/ppermute | solution.py:31
  160.4 0.9 collective-permute-done.19.refs_5_
  161.3 2.1 shard_map.77.refs_1_
  163.4 9.1 %collective-permute-start.30 = (bf16[29,8,64,128]{3,2,1,0:T(8,128)(2,1)}, bf16[29,8,64,128]{3,2,1,0:T(8,128)(2,1)}, u32[]{:S(2)}, u32[]{:S(2)}) collective-permute-start(bf16[29,8,64,128]{3,2,1,0:T(8,128)(2,1)} %shard_map.77.refs_1_), channel_id=1, source_target_pairs={{0,1},{1,0},{2,3},{3,2},{4,5},{5,4},{6,7},{7,6},{8,9},{9,8},{10,11... | collective-permute-start | bytes 11403272 | tf_op jit(solution)/shard_map/ppermute | solution.py:35
  172.5 8.4 %shard_map.78 = (bf16[64,2,8,464]{3,2,1,0:T(8,128)(2,1)S(1)}, f32[8,128]{1,0:T(8,128)S(1)}) custom-call(s32[8]{0:T(128)S(1)} %stack.35.refs_0_, bf16[29,8,64,128]{3,2,1,0:T(8,128)(2,1)} %shard_map.77.refs_1_, bf16[464,3712]{1,0:T(8,128)(2,1)S(1)} %copy-done, bf16[464,3712]{1,0:T(8,128)(2,1)} %collective-permute-done.5.refs_3_), custom_call_target="tpu_custom_call" | custom-call | bytes 15597568 | tf_op jit(solution)/shard_map/pallas_call | solution.py:60
  180.9 1.0 copy-done.2
  181.9 0.6 collective-permute-done.23.refs_1_
  182.5 2.1 shard_map.79
  184.7 0.6 copy-done.6
  185.2 3.5 %collective-permute-start.27 = (bf16[29,6,64,128]{3,2,1,0:T(8,128)(2,1)}, bf16[29,6,64,128]{3,2,1,0:T(8,128)(2,1)}, u32[]{:S(2)}, u32[]{:S(2)}) collective-permute-start(bf16[29,6,64,128]{3,2,1,0:T(8,128)(2,1)} %get-tuple-element.76.refs_1_), channel_id=1, source_target_pairs={{0,1},{1,0},{2,3},{3,2},{4,5},{5,4},{6,7},{7,6},{8,9},{9,8},{10,11... | collective-permute-start | bytes 8552456 | tf_op jit(solution)/shard_map/ppermute | solution.py:35
  188.8 0.6 collective-permute-start.25
  189.4 2.1 collective-permute-start.26
  191.5 5.6 %all-to-all-start.1 = ((bf16[64,2,8,464]{3,2,1,0:T(8,128)(2,1)}), bf16[64,2,8,464]{3,2,1,0:T(8,128)(2,1)S(1)}, u32[]{:S(2)}, u32[]{:S(2)}) async-start(bf16[64,2,8,464]{3,2,1,0:T(8,128)(2,1)} %shard_map.80), calls=%async_computation.1 | async-start | bytes 2097152 | tf_op jit(solution)/shard_map/all_to_all | solution.py:154
  197.0 5.7 %collective-permute-done.25.refs_2_ = bf16[29,64,128]{2,1,0:T(8,128)(2,1)S(1)} collective-permute-done((bf16[29,64,128]{2,1,0:T(8,128)(2,1)}, bf16[29,64,128]{2,1,0:T(8,128)(2,1)S(1)}, u32[]{:S(2)}, u32[]{:S(2)}) %collective-permute-start.25) | collective-permute-done | bytes 475168 | tf_op jit(solution)/shard_map/ppermute | solution.py:31
  202.7 1.2 collective-permute-start.28
  203.9 0.9 collective-permute-start.29
  204.8 7.2 %shard_map.81 = (f32[464,3712]{1,0:T(8,128)}, f32[8,128]{1,0:T(8,128)S(1)}) custom-call(bf16[464,1024]{1,0:T(8,128)(2,1)S(1)} %get-tuple-element.68.refs_6_.refs_0_, bf16[29,8,64,128]{3,2,1,0:T(8,128)(2,1)} %shard_map.77.refs_1_, bf16[29,8,64,128]{3,2,1,0:T(8,128)(2,1)} %collective-permute-done.30.refs_2_, f32[8,128]{1,0:T(8,128)S(1)} %get-tuple-element.74.refs_3_), custom_call_target="tpu_custom_call" | custom-call | tf_op jit(solution)/shard_map/pallas_call | solution.py:60
  212.0 8.3 %shard_map.82 = (f32[464,3712]{1,0:T(8,128)}, f32[8,128]{1,0:T(8,128)S(1)}) custom-call(bf16[464,1024]{1,0:T(8,128)(2,1)S(1)} %get-tuple-element.69.refs_7_.refs_0_, bf16[29,6,64,128]{3,2,1,0:T(8,128)(2,1)} %get-tuple-element.76.refs_1_, bf16[29,64,128]{2,1,0:T(8,128)(2,1)S(1)} %collective-permute-done.25.refs_2_, ...), custom_call_target="tpu_custom_call" | custom-call | tf_op jit(solution)/shard_map/pallas_call | solution.py:60
  220.3 0.9 shard_map.83
  (34 shorter events, 0.5 us)
Async XLA Ops:
  0.6 45.4 %collective-permute-start = (bf16[464,3712]{1,0:T(8,128)(2,1)}, bf16[464,3712]{1,0:T(8,128)(2,1)}, u32[]{:S(2)}, u32[]{:S(2)}) collective-permute-start(bf16[464,3712]{1,0:T(8,128)(2,1)} %bitcast.11), channel_id=1, source_target_pairs={{0,1},{1,0},{2,3},{3,2},{4,5},{5,4},{6,7},{7,6},{8,9},{9,8},{10,11... | collective-permute-start | bytes 10334216 | tf_op jit(solution)/shard_map/ppermute | solution.py:35
  2.1 53.6 %collective-permute-start.5 = (bf16[464,3712]{1,0:T(8,128)(2,1)}, bf16[464,3712]{1,0:T(8,128)(2,1)}, u32[]{:S(2)}, u32[]{:S(2)}) collective-permute-start(bf16[464,3712]{1,0:T(8,128)(2,1)} %refs_2_.5), channel_id=1, source_target_pairs={{0,1},{1,0},{2,3},{3,2},{4,5},{5,4},{6,7},{7,6},{8,9},{9,8},{10,11... | collective-permute-start | bytes 10334216 | tf_op jit(solution)/shard_map/ppermute | solution.py:35
  2.2 0.9 copy-start.4
  3.1 0.9 copy-start.5
  4.6 1.3 copy-start.1
  5.9 40.1 %all-to-all-start = ((bf16[64,4,8,464]{3,2,1,0:T(8,128)(2,1)}), bf16[64,4,8,464]{3,2,1,0:T(8,128)(2,1)S(1)}, u32[]{:S(2)}, u32[]{:S(2)}) async-start(bf16[64,4,8,464]{3,2,1,0:T(8,128)(2,1)} %copy-done.1), calls=%async_computation | async-start | bytes 4194304 | tf_op jit(solution)/shard_map/all_to_all | solution.py:154
  46.0 9.7 %copy-start = (bf16[464,3712]{1,0:T(8,128)(2,1)S(1)}, bf16[464,3712]{1,0:T(8,128)(2,1)}, u32[]{:S(2)}) copy-start(bf16[464,3712]{1,0:T(8,128)(2,1)} %refs_2_.5) | copy-start | bytes 10334212
  46.0 2.1 copy-start.3
  55.4 40.8 %collective-permute-start.1 = (bf16[29,4,64,128]{3,2,1,0:T(8,128)(2,1)S(1)}, bf16[29,4,64,128]{3,2,1,0:T(8,128)(2,1)S(1)}, u32[]{:S(2)}, u32[]{:S(2)}) collective-permute-start(bf16[29,4,64,128]{3,2,1,0:T(8,128)(2,1)S(1)} %get-tuple-element.44), channel_id=1, source_target_pairs={{0,8},{8,0},{1,9},{9,1},{2,10},{10,2},{3,11},{11,3},{4,12},{12,4},... | collective-permute-start | bytes 5701640 | tf_op jit(solution)/shard_map/ppermute | solution.py:35
  63.0 11.3 %collective-permute-start.8 = (bf16[29,64,128]{2,1,0:T(8,128)(2,1)S(1)}, bf16[29,64,128]{2,1,0:T(8,128)(2,1)S(1)}, u32[]{:S(2)}, u32[]{:S(2)}) collective-permute-start(bf16[29,64,128]{2,1,0:T(8,128)(2,1)S(1)} %get-tuple-element.55), channel_id=1, source_target_pairs={{0,2},{2,4},{4,6},{6,0},{1,3},{3,5},{5,7},{7,1},{8,10},{10,12},{12... | collective-permute-start | bytes 1425416 | tf_op jit(solution)/shard_map/ppermute | solution.py:31
  63.2 11.1 %collective-permute-start.9 = (bf16[29,64,128]{2,1,0:T(8,128)(2,1)S(1)}, bf16[29,64,128]{2,1,0:T(8,128)(2,1)S(1)}, u32[]{:S(2)}, u32[]{:S(2)}) collective-permute-start(bf16[29,64,128]{2,1,0:T(8,128)(2,1)S(1)} %get-tuple-element.56), channel_id=1, source_target_pairs={{0,6},{2,0},{4,2},{6,4},{1,7},{3,1},{5,3},{7,5},{8,14},{10,8},{12,... | collective-permute-start | bytes 1425416 | tf_op jit(solution)/shard_map/ppermute | solution.py:31
  65.7 34.1 %collective-permute-start.6 = (bf16[29,64,128]{2,1,0:T(8,128)(2,1)S(1)}, bf16[29,64,128]{2,1,0:T(8,128)(2,1)S(1)}, u32[]{:S(2)}, u32[]{:S(2)}) collective-permute-start(bf16[29,64,128]{2,1,0:T(8,128)(2,1)S(1)} %get-tuple-element.51), channel_id=1, source_target_pairs={{0,6},{2,0},{4,2},{6,4},{1,7},{3,1},{5,3},{7,5},{8,14},{10,8},{12,... | collective-permute-start | bytes 1425416 | tf_op jit(solution)/shard_map/ppermute | solution.py:31
  65.7 34.1 %collective-permute-start.7 = (bf16[29,64,128]{2,1,0:T(8,128)(2,1)S(1)}, bf16[29,64,128]{2,1,0:T(8,128)(2,1)S(1)}, u32[]{:S(2)}, u32[]{:S(2)}) collective-permute-start(bf16[29,64,128]{2,1,0:T(8,128)(2,1)S(1)} %get-tuple-element.52), channel_id=1, source_target_pairs={{0,2},{2,4},{4,6},{6,0},{1,3},{3,5},{5,7},{7,1},{8,10},{10,12},{12... | collective-permute-start | bytes 1425416 | tf_op jit(solution)/shard_map/ppermute | solution.py:31
  74.7 25.1 %collective-permute-start.10 = (bf16[29,64,128]{2,1,0:T(8,128)(2,1)S(1)}, bf16[29,64,128]{2,1,0:T(8,128)(2,1)S(1)}, u32[]{:S(2)}, u32[]{:S(2)}) collective-permute-start(bf16[29,64,128]{2,1,0:T(8,128)(2,1)S(1)} %get-tuple-element.59), channel_id=1, source_target_pairs={{0,2},{2,4},{4,6},{6,0},{1,3},{3,5},{5,7},{7,1},{8,10},{10,12},{12... | collective-permute-start | bytes 1425416 | tf_op jit(solution)/shard_map/ppermute | solution.py:31
  75.0 24.8 %collective-permute-start.11 = (bf16[29,64,128]{2,1,0:T(8,128)(2,1)S(1)}, bf16[29,64,128]{2,1,0:T(8,128)(2,1)S(1)}, u32[]{:S(2)}, u32[]{:S(2)}) collective-permute-start(bf16[29,64,128]{2,1,0:T(8,128)(2,1)S(1)} %get-tuple-element.60), channel_id=1, source_target_pairs={{0,6},{2,0},{4,2},{6,4},{1,7},{3,1},{5,3},{7,5},{8,14},{10,8},{12,... | collective-permute-start | bytes 1425416 | tf_op jit(solution)/shard_map/ppermute | solution.py:31
  96.2 17.8 %collective-permute-start.14 = (bf16[512,1024]{1,0:T(8,128)(2,1)S(1)}, bf16[512,1024]{1,0:T(8,128)(2,1)S(1)}, u32[]{:S(2)}, u32[]{:S(2)}) collective-permute-start(bf16[512,1024]{1,0:T(8,128)(2,1)S(1)} %get-tuple-element.65), channel_id=1, source_target_pairs={{0,1},{1,0},{2,3},{3,2},{4,5},{5,4},{6,7},{7,6},{8,9},{9,8},{10,11... | collective-permute-start | bytes 3145736 | tf_op jit(solution)/shard_map/ppermute | solution.py:35
  100.3 12.6 %collective-permute-start.12 = (bf16[29,64,128]{2,1,0:T(8,128)(2,1)S(1)}, bf16[29,64,128]{2,1,0:T(8,128)(2,1)S(1)}, u32[]{:S(2)}, u32[]{:S(2)}) collective-permute-start(bf16[29,64,128]{2,1,0:T(8,128)(2,1)S(1)} %get-tuple-element.62), channel_id=1, source_target_pairs={{0,8},{8,0},{1,9},{9,1},{2,10},{10,2},{3,11},{11,3},{4,12},{12,4},... | collective-permute-start | bytes 1425416 | tf_op jit(solution)/shard_map/ppermute | solution.py:35
  100.7 23.6 %collective-permute-start.2 = (bf16[29,64,128]{2,1,0:T(8,128)(2,1)S(1)}, bf16[29,64,128]{2,1,0:T(8,128)(2,1)S(1)}, u32[]{:S(2)}, u32[]{:S(2)}) collective-permute-start(bf16[29,64,128]{2,1,0:T(8,128)(2,1)S(1)} %get-tuple-element.46), channel_id=1, source_target_pairs={{0,2},{2,4},{4,6},{6,0},{1,3},{3,5},{5,7},{7,1},{8,10},{10,12},{12... | collective-permute-start | bytes 1425416 | tf_op jit(solution)/shard_map/ppermute | solution.py:31
  100.8 23.5 %collective-permute-start.3 = (bf16[29,64,128]{2,1,0:T(8,128)(2,1)S(1)}, bf16[29,64,128]{2,1,0:T(8,128)(2,1)S(1)}, u32[]{:S(2)}, u32[]{:S(2)}) collective-permute-start(bf16[29,64,128]{2,1,0:T(8,128)(2,1)S(1)} %get-tuple-element.47), channel_id=1, source_target_pairs={{0,6},{2,0},{4,2},{6,4},{1,7},{3,1},{5,3},{7,5},{8,14},{10,8},{12,... | collective-permute-start | bytes 1425416 | tf_op jit(solution)/shard_map/ppermute | solution.py:31
  103.4 20.9 %collective-permute-start.4 = (bf16[29,64,128]{2,1,0:T(8,128)(2,1)S(1)}, bf16[29,64,128]{2,1,0:T(8,128)(2,1)S(1)}, u32[]{:S(2)}, u32[]{:S(2)}) collective-permute-start(bf16[29,64,128]{2,1,0:T(8,128)(2,1)S(1)} %get-tuple-element.48), channel_id=1, source_target_pairs={{0,4},{2,6},{4,0},{6,2},{1,5},{3,7},{5,1},{7,3},{8,12},{10,14},{12... | collective-permute-start | bytes 1425416 | tf_op jit(solution)/shard_map/ppermute | solution.py:31
  113.6 11.7 %collective-permute-start.13 = (bf16[29,64,128]{2,1,0:T(8,128)(2,1)S(1)}, bf16[29,64,128]{2,1,0:T(8,128)(2,1)S(1)}, u32[]{:S(2)}, u32[]{:S(2)}) collective-permute-start(bf16[29,64,128]{2,1,0:T(8,128)(2,1)S(1)} %get-tuple-element.64.refs_4_), channel_id=1, source_target_pairs={{0,8},{8,0},{1,9},{9,1},{2,10},{10,2},{3,11},{11,3},{4,12},{12,4},... | collective-permute-start | bytes 1425416 | tf_op jit(solution)/shard_map/ppermute | solution.py:35
  125.7 10.8 %collective-permute-start.15 = (bf16[29,64,128]{2,1,0:T(8,128)(2,1)S(1)}, bf16[29,64,128]{2,1,0:T(8,128)(2,1)S(1)}, u32[]{:S(2)}, u32[]{:S(2)}) collective-permute-start(bf16[29,64,128]{2,1,0:T(8,128)(2,1)S(1)} %shard_map.74.refs_0_), channel_id=1, source_target_pairs={{0,8},{8,0},{1,9},{9,1},{2,10},{10,2},{3,11},{11,3},{4,12},{12,4},... | collective-permute-start | bytes 1425416 | tf_op jit(solution)/shard_map/ppermute | solution.py:35
  126.1 11.6 %collective-permute-start.16 = (bf16[29,64,128]{2,1,0:T(8,128)(2,1)S(1)}, bf16[29,64,128]{2,1,0:T(8,128)(2,1)S(1)}, u32[]{:S(2)}, u32[]{:S(2)}) collective-permute-start(bf16[29,64,128]{2,1,0:T(8,128)(2,1)S(1)} %shard_map.74.refs_0_), channel_id=1, source_target_pairs={{0,2},{2,4},{4,6},{6,0},{1,3},{3,5},{5,7},{7,1},{8,10},{10,12},{12... | collective-permute-start | bytes 1425416 | tf_op jit(solution)/shard_map/ppermute | solution.py:31
  126.5 11.2 %collective-permute-start.17 = (bf16[29,64,128]{2,1,0:T(8,128)(2,1)S(1)}, bf16[29,64,128]{2,1,0:T(8,128)(2,1)S(1)}, u32[]{:S(2)}, u32[]{:S(2)}) collective-permute-start(bf16[29,64,128]{2,1,0:T(8,128)(2,1)S(1)} %shard_map.74.refs_0_), channel_id=1, source_target_pairs={{0,6},{2,0},{4,2},{6,4},{1,7},{3,1},{5,3},{7,5},{8,14},{10,8},{12,... | collective-permute-start | bytes 1425416 | tf_op jit(solution)/shard_map/ppermute | solution.py:31
  128.8 20.1 %collective-permute-start.18 = (bf16[29,64,128]{2,1,0:T(8,128)(2,1)S(1)}, bf16[29,64,128]{2,1,0:T(8,128)(2,1)S(1)}, u32[]{:S(2)}, u32[]{:S(2)}) collective-permute-start(bf16[29,64,128]{2,1,0:T(8,128)(2,1)S(1)} %shard_map.74.refs_0_), channel_id=1, source_target_pairs={{0,4},{2,6},{4,0},{6,2},{1,5},{3,7},{5,1},{7,3},{8,12},{10,14},{12... | collective-permute-start | bytes 1425416 | tf_op jit(solution)/shard_map/ppermute | solution.py:31
  149.0 12.3 %collective-permute-start.19 = (bf16[12,3,64,128]{3,2,1,0:T(8,128)(2,1)S(1)}, bf16[12,3,64,128]{3,2,1,0:T(8,128)(2,1)S(1)}, u32[]{:S(2)}, u32[]{:S(2)}) collective-permute-start(bf16[12,3,64,128]{3,2,1,0:T(8,128)(2,1)S(1)} %get-tuple-element.70), channel_id=1, source_target_pairs={{0,8},{8,0},{1,9},{9,1},{2,10},{10,2},{3,11},{11,3},{4,12},{12,4},... | collective-permute-start | bytes 1769480 | tf_op jit(solution)/shard_map/ppermute | solution.py:35
  149.4 6.6 %collective-permute-start.20 = (bf16[17,64,128]{2,1,0:T(8,128)(2,1)S(1)}, bf16[17,64,128]{2,1,0:T(8,128)(2,1)S(1)}, u32[]{:S(2)}, u32[]{:S(2)}) collective-permute-start(bf16[17,64,128]{2,1,0:T(8,128)(2,1)S(1)} %get-tuple-element.71), channel_id=1, source_target_pairs={{0,2},{2,4},{4,6},{6,0},{1,3},{3,5},{5,7},{7,1},{8,10},{10,12},{12... | collective-permute-start | bytes 835592 | tf_op jit(solution)/shard_map/ppermute | solution.py:31
  150.0 8.1 %collective-permute-start.21 = (bf16[17,64,128]{2,1,0:T(8,128)(2,1)S(1)}, bf16[17,64,128]{2,1,0:T(8,128)(2,1)S(1)}, u32[]{:S(2)}, u32[]{:S(2)}) collective-permute-start(bf16[17,64,128]{2,1,0:T(8,128)(2,1)S(1)} %get-tuple-element.71), channel_id=1, source_target_pairs={{0,6},{2,0},{4,2},{6,4},{1,7},{3,1},{5,3},{7,5},{8,14},{10,8},{12,... | collective-permute-start | bytes 835592 | tf_op jit(solution)/shard_map/ppermute | solution.py:31
  152.1 8.3 %collective-permute-start.22 = (bf16[17,64,128]{2,1,0:T(8,128)(2,1)S(1)}, bf16[17,64,128]{2,1,0:T(8,128)(2,1)S(1)}, u32[]{:S(2)}, u32[]{:S(2)}) collective-permute-start(bf16[17,64,128]{2,1,0:T(8,128)(2,1)S(1)} %get-tuple-element.71), channel_id=1, source_target_pairs={{0,4},{2,6},{4,0},{6,2},{1,5},{3,7},{5,1},{7,3},{8,12},{10,14},{12... | collective-permute-start | bytes 835592 | tf_op jit(solution)/shard_map/ppermute | solution.py:31
  152.1 30.4 %collective-permute-start.23 = (bf16[29,2,64,128]{3,2,1,0:T(8,128)(2,1)S(1)}, bf16[29,2,64,128]{3,2,1,0:T(8,128)(2,1)S(1)}, u32[]{:S(2)}, u32[]{:S(2)}) collective-permute-start(bf16[29,2,64,128]{3,2,1,0:T(8,128)(2,1)S(1)} %get-tuple-element.73.refs_0_), channel_id=1, source_target_pairs={{0,2},{2,4},{4,6},{6,0},{1,3},{3,5},{5,7},{7,1},{8,10},{10,12},{12... | collective-permute-start | bytes 2850824 | tf_op jit(solution)/shard_map/ppermute | solution.py:31
  156.0 26.5 %collective-permute-start.24 = (bf16[29,2,64,128]{3,2,1,0:T(8,128)(2,1)S(1)}, bf16[29,2,64,128]{3,2,1,0:T(8,128)(2,1)S(1)}, u32[]{:S(2)}, u32[]{:S(2)}) collective-permute-start(bf16[29,2,64,128]{3,2,1,0:T(8,128)(2,1)S(1)} %get-tuple-element.73.refs_0_), channel_id=1, source_target_pairs={{0,6},{2,0},{4,2},{6,4},{1,7},{3,1},{5,3},{7,5},{8,14},{10,8},{12,... | collective-permute-start | bytes 2850824 | tf_op jit(solution)/shard_map/ppermute | solution.py:31
  163.4 41.4 %collective-permute-start.30 = (bf16[29,8,64,128]{3,2,1,0:T(8,128)(2,1)}, bf16[29,8,64,128]{3,2,1,0:T(8,128)(2,1)}, u32[]{:S(2)}, u32[]{:S(2)}) collective-permute-start(bf16[29,8,64,128]{3,2,1,0:T(8,128)(2,1)} %shard_map.77.refs_1_), channel_id=1, source_target_pairs={{0,1},{1,0},{2,3},{3,2},{4,5},{5,4},{6,7},{7,6},{8,9},{9,8},{10,11... | collective-permute-start | bytes 11403272 | tf_op jit(solution)/shard_map/ppermute | solution.py:35
  180.9 1.0 copy-start.2
  184.7 0.6 copy-start.6
  185.2 26.8 %collective-permute-start.27 = (bf16[29,6,64,128]{3,2,1,0:T(8,128)(2,1)}, bf16[29,6,64,128]{3,2,1,0:T(8,128)(2,1)}, u32[]{:S(2)}, u32[]{:S(2)}) collective-permute-start(bf16[29,6,64,128]{3,2,1,0:T(8,128)(2,1)} %get-tuple-element.76.refs_1_), channel_id=1, source_target_pairs={{0,1},{1,0},{2,3},{3,2},{4,5},{5,4},{6,7},{7,6},{8,9},{9,8},{10,11... | collective-permute-start | bytes 8552456 | tf_op jit(solution)/shard_map/ppermute | solution.py:35
  188.8 13.9 %collective-permute-start.25 = (bf16[29,64,128]{2,1,0:T(8,128)(2,1)}, bf16[29,64,128]{2,1,0:T(8,128)(2,1)S(1)}, u32[]{:S(2)}, u32[]{:S(2)}) collective-permute-start(bf16[29,64,128]{2,1,0:T(8,128)(2,1)} %get-tuple-element.77), channel_id=1, source_target_pairs={{0,2},{2,4},{4,6},{6,0},{1,3},{3,5},{5,7},{7,1},{8,10},{10,12},{12... | collective-permute-start | bytes 1425416 | tf_op jit(solution)/shard_map/ppermute | solution.py:31
  189.4 14.5 %collective-permute-start.26 = (bf16[29,64,128]{2,1,0:T(8,128)(2,1)}, bf16[29,64,128]{2,1,0:T(8,128)(2,1)}, u32[]{:S(2)}, u32[]{:S(2)}) collective-permute-start(bf16[29,64,128]{2,1,0:T(8,128)(2,1)} %get-tuple-element.78), channel_id=1, source_target_pairs={{0,6},{2,0},{4,2},{6,4},{1,7},{3,1},{5,3},{7,5},{8,14},{10,8},{12,... | collective-permute-start | bytes 1425416 | tf_op jit(solution)/shard_map/ppermute | solution.py:31
  191.5 28.9 %all-to-all-start.1 = ((bf16[64,2,8,464]{3,2,1,0:T(8,128)(2,1)}), bf16[64,2,8,464]{3,2,1,0:T(8,128)(2,1)S(1)}, u32[]{:S(2)}, u32[]{:S(2)}) async-start(bf16[64,2,8,464]{3,2,1,0:T(8,128)(2,1)} %shard_map.80), calls=%async_computation.1 | async-start | bytes 2097152 | tf_op jit(solution)/shard_map/all_to_all | solution.py:154
  202.7 9.3 %collective-permute-start.28 = (bf16[29,64,128]{2,1,0:T(8,128)(2,1)S(1)}, bf16[29,64,128]{2,1,0:T(8,128)(2,1)S(1)}, u32[]{:S(2)}, u32[]{:S(2)}) collective-permute-start(bf16[29,64,128]{2,1,0:T(8,128)(2,1)S(1)} %collective-permute-done.25.refs_2_), channel_id=1, source_target_pairs={{0,1},{1,0},{2,3},{3,2},{4,5},{5,4},{6,7},{7,6},{8,9},{9,8},{10,11... | collective-permute-start | bytes 1425416 | tf_op jit(solution)/shard_map/ppermute | solution.py:35
  203.9 8.1 %collective-permute-start.29 = (bf16[29,64,128]{2,1,0:T(8,128)(2,1)}, bf16[29,64,128]{2,1,0:T(8,128)(2,1)S(1)}, u32[]{:S(2)}, u32[]{:S(2)}) collective-permute-start(bf16[29,64,128]{2,1,0:T(8,128)(2,1)} %collective-permute-done.26.refs_3_), channel_id=1, source_target_pairs={{0,1},{1,0},{2,3},{3,2},{4,5},{5,4},{6,7},{7,6},{8,9},{9,8},{10,11... | collective-permute-start | bytes 1425416 | tf_op jit(solution)/shard_map/ppermute | solution.py:35
where the time goes:
time: 222 us; the launch traced here: 221 us
  waiting for transfers between devices  109 us (49%)
  starting transfers between devices  57.3 us (26%)
  Pallas kernels  47.2 us (21%)
  local copies, waits for them, and re-layouts  6.87 us (3%)
    pallas_call x16, Pallas kernels, call(): pl.pallas_call(run, out_shape=[jax.ShapeDtypeStruct(s, d) for s, d in out...  47.2 us
    ppermute x19, waiting for transfers between devices, ring(): lax.ppermute(v, axis, [(i, (i + step) % 4) for i in range(4)])  43.8 us
    ppermute x12, waiting for transfers between devices, swap(): return lambda v: lax.ppermute(v, axis, [(0, 1), (1, 0)])  36.3 us
    all_to_all x2, waiting for transfers between devices, exchange(): lax.all_to_all(v, ('z', 'yh', 'y', 'x'), split_axis=0, concat_axis=0, til...  28.7 us
    ppermute x12, starting transfers between devices, swap(): return lambda v: lax.ppermute(v, axis, [(0, 1), (1, 0)])  21.4 us
    ppermute x19, starting transfers between devices, ring(): lax.ppermute(v, axis, [(i, (i + step) % 4) for i in range(4)])  19.2 us
    all_to_all x2, starting transfers between devices, exchange(): lax.all_to_all(v, ('z', 'yh', 'y', 'x'), split_axis=0, concat_axis=0, til...  16.8 us
    unnamed x14, local copies, waits for them, and re-layouts  6.79 us
  transfers between devices with their start and end apart: 33, of which 15 were waited for; matrix products, arithmetic and copies ran while one was open for 0% of the time, Pallas kernels for 21%

commit v1 on v0

--- a/solution.py
+++ b/solution.py
@@ -13,8 +13,9 @@
 inv_root_two_pi = 0.3989422804014327
 AXES = ("z", "yh", "y", "x", "core")
 TILE = 128
-SPLIT_DH = 17
-WIDTH = 4
+SPLIT_DH = 14
+MOVED = 5
+WIDTH = 8
 WIDE = 8
 bf16, f32 = jnp.bfloat16, jnp.float32
 
@@ -154,7 +155,8 @@
     return lax.all_to_all(v, ("z", "yh", "y", "x"), split_axis=0, concat_axis=0, tiled=True)
 
 
-def product_body(ring_first, order, *refs):
+def product_body(ring_first, moved, order, *refs):
+    extra, refs = refs[:ring_first], refs[ring_first:]
     got, *sources, own, sib = refs[:5]
     *outs, left, weight, sems = refs[5:]
     weights = Streamed(sources, weight, sems, WIDTH)
@@ -179,20 +181,35 @@
                 for k, ref in enumerate(outs):
                     ref[tile + j] = part[k]
             else:
-                for dy, ref in enumerate(outs):
-                    ref[tile + j] = part[4 * dy : 4 * dy + 4]
-
-    groups(outs[0].shape[0], WIDTH, multiply)
-
-
-def product(order, got, w_own, w_sib, ring_first, after=()):
+                for dy in range(2):
+                    outs[dy][tile + j] = part[4 * dy : 4 * dy + 4]
+
+    if ring_first:
+        groups(weights.count, WIDTH, multiply)
+        for k, ref in enumerate(outs):
+            ref[weights.count :] = extra[0][:, k]
+    else:
+        rest = weights.count - moved
+        groups(rest, WIDTH, multiply)
+        weights.wait(rest, moved)
+        cols = slice(rest * TILE, weights.count * TILE)
+        total = dot(left[...], weight[:, cols], ((1,), (0,))).astype(bf16)
+        total = total.reshape(8, rows, moved * TILE)
+        for j in range(moved):
+            outs[2][j] = total[:, :, j * TILE : (j + 1) * TILE]
+
+
+def product(order, got, w_own, w_sib, extra=(), after=()):
     rows, feats = 8 * got.shape[2], got.shape[3]
     nt = w_own.shape[1] // TILE
-    outs = [((nt, rows, TILE), bf16)] * 8 if ring_first else [((nt, 4, rows, TILE), bf16)] * 2
+    if extra:
+        outs = [((nt + MOVED, rows, TILE), bf16)] * 8
+    else:
+        outs = [((nt - MOVED, 4, rows, TILE), bf16)] * 2 + [((MOVED, 8, rows, TILE), bf16)]
     return call(
-        functools.partial(product_body, ring_first),
+        functools.partial(product_body, len(extra), MOVED),
         [((8 * rows, feats), bf16)] * 2 + outs,
-        [order, got, w_own, w_sib],
+        [order, *extra, got, w_own, w_sib],
         [
             ((8 * rows, 2 * roomy(feats)), bf16),
             ((2 * roomy(feats), nt * TILE), bf16),
@@ -246,11 +263,18 @@
     tiles(act.shape[0], step)
 
 
-def slope_body(kept, r, l, x, slope, out):
+def slope_body(kept, r, l, x, kept_ring, y, slope, out):
+    first = kept.shape[0]
+
     def step(t):
         out[t] = (add(kept[t], r[t], l[t], x[t]) * slope[t]).astype(bf16)
 
-    tiles(out.shape[0], step)
+    def moved_step(i):
+        t, at = first + i, out.shape[0] + i
+        out[t] = (add(kept_ring[at], y[at]) * slope[t]).astype(bf16)
+
+    tiles(first, step)
+    tiles(out.shape[0] - first, moved_step)
 
 
 def gather_first(v):
@@ -279,7 +303,12 @@
     return (*state, over(to_over), up(to_ring), down(to_ring), far(to_ring)), pair
 
 
-def whole_body(v, y, r, l, x, y2, r2, l2, x2, out):
+def whole_body(v, y, r, l, x, y2, r2, l2, x2, *outs):
+    for out in outs:
+        place_whole(v, y, r, l, x, y2, r2, l2, x2, out)
+
+
+def place_whole(v, y, r, l, x, y2, r2, l2, x2, out):
     na = r2.shape[0]
     for k, ref in enumerate((v, l, x, r, y)):
         out[:, k] = ref[...]
@@ -290,8 +319,8 @@
 
 def gather_end(state):
     nt, rows, _ = state[0].shape
-    whole = call(whole_body, [((nt, 8, rows, TILE), bf16)], state)[0]
-    return whole, swap("core")(whole)
+    now, later = call(whole_body, [((nt, 8, rows, TILE), bf16)] * 2, state)
+    return now, later, swap("core")(later)
 
 
 def forward_body(pair, r, l, up, down, near):
@@ -438,44 +467,45 @@
     both = exchange(both)
 
     up, down, far, over = x_links()
-    g_own, g_sib, keep_g, to_over = product(order, both, w_out, w_out_sib, False)
+    g_own, g_sib, keep_g, to_over, moved = product(order, both, w_out, w_out_sib)
     got_g = over(to_over)
-    x_own, x_sib, *parts = product(order, both, w_in, w_in_sib, True, (keep_g,))
+    x_own, x_sib, *parts = product(order, both, w_in, w_in_sib, (moved,), (keep_g,))
     r, l = up(parts[2]), down(parts[6])
     l_near, r_near = down(parts[3]), up(parts[5])
-    one = (nt, rows, TILE)
+    one, more, less = ((n, rows, TILE) for n in (nt, nt + MOVED, nt - MOVED))
     to_up, to_down, sibs = call(
         ring_forward_body,
-        [(one, bf16)] * 2 + [((8 * rows, 2 * roomy(feats)), bf16)],
+        [(more, bf16)] * 2 + [((8 * rows, 2 * roomy(feats)), bf16)],
         (parts[1], parts[7], r, l, x_sib, g_sib),
     )
     r_far, l_far = up(to_up), down(to_down)
     kept_g, to_up, to_far, to_down = call(
-        across_sum_body, [(one, f32)] + [(one, bf16)] * 3, (keep_g, got_g)
+        across_sum_body, [(less, f32)] + [(less, bf16)] * 3, (keep_g, got_g)
     )
     got_g = up(to_up), down(to_down), far(to_far)
     swapped = cc(sibs)
     kept, sent = call(
         ring_sum_body,
-        [(one, f32), (one, bf16)],
+        [(more, f32), (more, bf16)],
         (parts[0], parts[4], l_near, r_near, r_far, l_far),
         after=(kept_g,),
     )
-    act, slope = call(act_body, [(one, bf16), (one, f32)], (kept, over(sent)))
+    y = over(sent)
+    act, slope = call(act_body, [(one, bf16), (one, f32)], (kept, y), after=got_g[:1])
     act_across = over(act)
-    dh = call(slope_body, [(one, bf16)], (kept_g, *got_g, slope), after=(act_across, swapped))[0]
+    dh = call(slope_body, [(one, bf16)], (kept_g, *got_g, kept, y, slope), after=(swapped,))[0]
     x_turned, g_turned = call(
         transposed_body, [((feats, 16 * rows), bf16)] * 2, (x_own, g_own, swapped)
     )
     state_d, act_pair = gather_second(
         gather_first(dh), SPLIT_DH, act, act_across, (x_turned, g_turned)
     )
-    dh_own, dh_sib = gather_end(state_d)
+    dh_now, dh_own, dh_sib = gather_end(state_d)
 
     gx, token = call(
         input_grad_body,
         [((64, 2, tokens, feats), bf16)],
-        (order, dh_own, w_in, w_in_sib),
+        (order, dh_now, w_in, w_in_sib),
         [((8 * rows, 2 * roomy(feats)), f32), ((2 * roomy(feats), nt * TILE), bf16)],
         smem=1,
         token=True,

time: 222 us -> 210 us (0.946)
  waiting for transfers between devices: 109 us -> 91.7 us
  starting transfers between devices: 57.3 us -> 64 us
  Pallas kernels: 47.2 us -> 44 us
    ppermute x12, waiting for transfers between devices: 36.3 us -> 17.5 us  [swap(): return lambda v: lax.ppermute(v, axis, [(0, 1), (1, 0)])]
    all_to_all x2, starting transfers between devices: 16.8 us -> 20.5 us  [exchange(): lax.all_to_all(v, ('z', 'yh', 'y', 'x'), split_axis=0, concat_axis=0, til...]
    pallas_call x16, Pallas kernels: 47.2 us -> 44 us  [call(): pl.pallas_call(run, out_shape=[jax.ShapeDtypeStruct(s, d) for s, d in out...]
  transfers between devices with their start and end apart: 33 -> 33, of which waited for: 15 -> 17; matrix products, arithmetic and copies ran while one was open for 0% -> 0% of each run, Pallas kernels for 21% -> 21%
where the time goes in v1:
time: 210 us; the launch traced here: 207 us
  waiting for transfers between devices  91.7 us (44%)
  starting transfers between devices  64 us (30%)
  Pallas kernels  44 us (21%)
  local copies, waits for them, and re-layouts  6.89 us (3%)
    ppermute x19, waiting for transfers between devices, ring(): lax.ppermute(v, axis, [(i, (i + step) % 4) for i in range(4)])  45.1 us
    pallas_call x16, Pallas kernels, call(): pl.pallas_call(run, out_shape=[jax.ShapeDtypeStruct(s, d) for s, d in out...  44 us
    all_to_all x2, waiting for transfers between devices, exchange(): lax.all_to_all(v, ('z', 'yh', 'y', 'x'), split_axis=0, concat_axis=0, til...  29.1 us
    ppermute x12, starting transfers between devices, swap(): return lambda v: lax.ppermute(v, axis, [(0, 1), (1, 0)])  23.1 us
    ppermute x19, starting transfers between devices, ring(): lax.ppermute(v, axis, [(i, (i + step) % 4) for i in range(4)])  20.5 us
    all_to_all x2, starting transfers between devices, exchange(): lax.all_to_all(v, ('z', 'yh', 'y', 'x'), split_axis=0, concat_axis=0, til...  20.5 us
    ppermute x12, waiting for transfers between devices, swap(): return lambda v: lax.ppermute(v, axis, [(0, 1), (1, 0)])  17.5 us
    unnamed x14, local copies, waits for them, and re-layouts  6.8 us
  transfers between devices with their start and end apart: 33, of which 17 were waited for; matrix products, arithmetic and copies ran while one was open for 0% of the time, Pallas kernels for 21%

profile of v1, /device:TPU:1, one launch (start us, length us, event | category | flops | bytes accessed | tf_op | source)
XLA Modules:
  0.0 207.5 jit_solution(1005459805997242211)
XLA Ops:
  0.6 1.5 collective-permute-start
  2.2 0.9 copy-done.4
  3.1 0.9 copy-done.5
  4.0 0.6 shard_map.67
  4.6 1.3 copy-done.1
  5.9 11.2 %all-to-all-start = ((bf16[64,4,8,464]{3,2,1,0:T(8,128)(2,1)}), bf16[64,4,8,464]{3,2,1,0:T(8,128)(2,1)S(1)}, u32[]{:S(2)}, u32[]{:S(2)}) async-start(bf16[64,4,8,464]{3,2,1,0:T(8,128)(2,1)} %copy-done.1), calls=%async_computation | async-start | bytes 4194304 | tf_op jit(solution)/shard_map/all_to_all | solution.py:155
  17.3 28.7 %all-to-all-done.refs_1_.refs_2_ = bf16[64,4,8,464]{3,2,1,0:T(8,128)(2,1)S(1)} async-done(((bf16[64,4,8,464]{3,2,1,0:T(8,128)(2,1)}), bf16[64,4,8,464]{3,2,1,0:T(8,128)(2,1)S(1)}, u32[]{:S(2)}, u32[]{:S(2)}) %all-to-all-start) | async-done | bytes 1900576 | tf_op jit(solution)/shard_map/all_to_all | solution.py:155
  46.0 2.1 %copy-done.3 = bf16[3712,464]{0,1:T(8,128)(2,1)S(1)} copy-done((bf16[3712,464]{0,1:T(8,128)(2,1)S(1)}, bf16[3712,464]{0,1:T(8,128)(2,1)}, u32[]{:S(2)}) %copy-start.3) | copy-done | bytes 3444760
  48.2 6.6 %shard_map.68 = (bf16[512,464]{1,0:T(8,128)(2,1)S(1)}, bf16[512,464]{1,0:T(8,128)(2,1)S(1)}, bf16[24,4,64,128]{3,2,1,0:T(8,128)(2,1)S(1)}, bf16[24,4,64,128]{3,2...) custom-call(s32[8]{0:T(128)S(1)} %stack.35.refs_0_, bf16[64,4,8,464]{3,2,1,0:T(8,128)(2,1)S(1)} %all-to-all-done.refs_1_.refs_2_, ...), custom_call_target="tpu_custom_call" | custom-call | bytes 17694720 | tf_op jit(solution)/shard_map/pallas_call | solution.py:61
  54.8 0.4 collective-permute-start.1
  55.2 6.7 %shard_map.70 = (bf16[512,464]{1,0:T(8,128)(2,1)S(1)}, bf16[512,464]{1,0:T(8,128)(2,1)S(1)}, bf16[34,64,128]{2,1,0:T(8,128)(2,1)S(1)}, bf16[34,64,128]{2,1,0:T(8...) custom-call(s32[8]{0:T(128)S(1)} %stack.35.refs_0_, ...), custom_call_target="tpu_custom_call" | custom-call | bytes 19005440 | tf_op jit(solution)/shard_map/pallas_call | solution.py:61
  62.0 2.6 %collective-permute-start.9 = (bf16[34,64,128]{2,1,0:T(8,128)(2,1)S(1)}, bf16[34,64,128]{2,1,0:T(8,128)(2,1)S(1)}, u32[]{:S(2)}, u32[]{:S(2)}) collective-permute-start(bf16[34,64,128]{2,1,0:T(8,128)(2,1)S(1)} %get-tuple-element.60), channel_id=1, source_target_pairs={{0,6},{2,0},{4,2},{6,4},{1,7},{3,1},{5,3},{7,5},{8,14},{10,8},{12,... | collective-permute-start | bytes 1671176 | tf_op jit(solution)/shard_map/ppermute | solution.py:32
  64.6 1.4 collective-permute-start.7
  66.1 8.9 %collective-permute-done.8.refs_2_ = bf16[34,64,128]{2,1,0:T(8,128)(2,1)S(1)} collective-permute-done((bf16[34,64,128]{2,1,0:T(8,128)(2,1)S(1)}, bf16[34,64,128]{2,1,0:T(8,128)(2,1)S(1)}, u32[]{:S(2)}, u32[]{:S(2)}) %collective-permute-start.8) | collective-permute-done | bytes 557088 | tf_op jit(solution)/shard_map/ppermute | solution.py:32
  74.9 0.5 shard_map.71
  75.7 2.4 %collective-permute-start.11 = (bf16[34,64,128]{2,1,0:T(8,128)(2,1)S(1)}, bf16[34,64,128]{2,1,0:T(8,128)(2,1)S(1)}, u32[]{:S(2)}, u32[]{:S(2)}) collective-permute-start(bf16[34,64,128]{2,1,0:T(8,128)(2,1)S(1)} %get-tuple-element.64), channel_id=1, source_target_pairs={{0,6},{2,0},{4,2},{6,4},{1,7},{3,1},{5,3},{7,5},{8,14},{10,8},{12,... | collective-permute-start | bytes 1671176 | tf_op jit(solution)/shard_map/ppermute | solution.py:32
  78.1 10.5 %collective-permute-done.1.refs_1_ = bf16[24,4,64,128]{3,2,1,0:T(8,128)(2,1)S(1)} collective-permute-done((bf16[24,4,64,128]{3,2,1,0:T(8,128)(2,1)S(1)}, bf16[24,4,64,128]{3,2,1,0:T(8,128)(2,1)S(1)}, u32[]{:S(2)}, u32[]{:S(2)}) %collective-permute-start.1) | collective-permute-done | bytes 1572896 | tf_op jit(solution)/shard_map/ppermute | solution.py:36
  88.6 3.1 %collective-permute-start.13 = (bf16[512,1024]{1,0:T(8,128)(2,1)S(1)}, bf16[512,1024]{1,0:T(8,128)(2,1)S(1)}, u32[]{:S(2)}, u32[]{:S(2)}) collective-permute-start(bf16[512,1024]{1,0:T(8,128)(2,1)S(1)} %get-tuple-element.68), channel_id=1, source_target_pairs={{0,1},{1,0},{2,3},{3,2},{4,5},{5,4},{6,7},{7,6},{8,9},{9,8},{10,11... | collective-permute-start | bytes 3145736 | tf_op jit(solution)/shard_map/ppermute | solution.py:36
  91.7 0.4 shard_map.69
  92.1 6.7 %collective-permute-done.10.refs_4_ = bf16[34,64,128]{2,1,0:T(8,128)(2,1)S(1)} collective-permute-done((bf16[34,64,128]{2,1,0:T(8,128)(2,1)S(1)}, bf16[34,64,128]{2,1,0:T(8,128)(2,1)S(1)}, u32[]{:S(2)}, u32[]{:S(2)}) %collective-permute-start.10) | collective-permute-done | bytes 557088 | tf_op jit(solution)/shard_map/ppermute | solution.py:32
  98.8 0.5 shard_map.72
  99.3 1.1 collective-permute-start.12
  100.8 2.3 %collective-permute-start.3 = (bf16[24,64,128]{2,1,0:T(8,128)(2,1)S(1)}, bf16[24,64,128]{2,1,0:T(8,128)(2,1)S(1)}, u32[]{:S(2)}, u32[]{:S(2)}) collective-permute-start(bf16[24,64,128]{2,1,0:T(8,128)(2,1)S(1)} %get-tuple-element.50), channel_id=1, source_target_pairs={{0,6},{2,0},{4,2},{6,4},{1,7},{3,1},{5,3},{7,5},{8,14},{10,8},{12,... | collective-permute-start | bytes 1179656 | tf_op jit(solution)/shard_map/ppermute | solution.py:32
  103.2 0.9 collective-permute-start.4
  104.1 4.6 %collective-permute-done.2.refs_2_.refs_1_ = bf16[24,64,128]{2,1,0:T(8,128)(2,1)S(1)} collective-permute-done((bf16[24,64,128]{2,1,0:T(8,128)(2,1)S(1)}, bf16[24,64,128]{2,1,0:T(8,128)(2,1)S(1)}, u32[]{:S(2)}, u32[]{:S(2)}) %collective-permute-start.2) | collective-permute-done | bytes 393248 | tf_op jit(solution)/shard_map/ppermute | solution.py:32
  108.7 1.6 collective-permute-done.12.refs_1_.refs_5_
  110.3 0.7 shard_map.73
  111.0 6.4 %collective-permute-done.4.refs_3_ = bf16[24,64,128]{2,1,0:T(8,128)(2,1)S(1)} collective-permute-done((bf16[24,64,128]{2,1,0:T(8,128)(2,1)S(1)}, bf16[24,64,128]{2,1,0:T(8,128)(2,1)S(1)}, u32[]{:S(2)}, u32[]{:S(2)}) %collective-permute-start.4) | collective-permute-done | bytes 393248 | tf_op jit(solution)/shard_map/ppermute | solution.py:32
  117.4 0.4 shard_map.74.refs_0_
  117.8 0.6 collective-permute-start.14
  118.4 0.6 collective-permute-start.15
  119.0 2.1 %collective-permute-start.16 = (bf16[29,64,128]{2,1,0:T(8,128)(2,1)S(1)}, bf16[29,64,128]{2,1,0:T(8,128)(2,1)S(1)}, u32[]{:S(2)}, u32[]{:S(2)}) collective-permute-start(bf16[29,64,128]{2,1,0:T(8,128)(2,1)S(1)} %shard_map.74.refs_0_), channel_id=1, source_target_pairs={{0,6},{2,0},{4,2},{6,4},{1,7},{3,1},{5,3},{7,5},{8,14},{10,8},{12,... | collective-permute-start | bytes 1425416 | tf_op jit(solution)/shard_map/ppermute | solution.py:32
  121.1 1.0 collective-permute-start.18
  122.0 0.6 shard_map.75
  122.7 2.7 %collective-permute-done.14.refs_0_.refs_1_ = bf16[29,64,128]{2,1,0:T(8,128)(2,1)S(1)} collective-permute-done((bf16[29,64,128]{2,1,0:T(8,128)(2,1)S(1)}, bf16[29,64,128]{2,1,0:T(8,128)(2,1)S(1)}, u32[]{:S(2)}, u32[]{:S(2)}) %collective-permute-start.14) | collective-permute-done | bytes 475168 | tf_op jit(solution)/shard_map/ppermute | solution.py:36
  125.4 3.4 %collective-permute-done.15.refs_1_.refs_2_ = bf16[29,64,128]{2,1,0:T(8,128)(2,1)S(1)} collective-permute-done((bf16[29,64,128]{2,1,0:T(8,128)(2,1)S(1)}, bf16[29,64,128]{2,1,0:T(8,128)(2,1)S(1)}, u32[]{:S(2)}, u32[]{:S(2)}) %collective-permute-start.15) | collective-permute-done | bytes 475168 | tf_op jit(solution)/shard_map/ppermute | solution.py:32
  128.8 0.7 collective-permute-done.16.refs_2_.refs_3_
  129.5 6.5 %collective-permute-done.17.refs_3_.refs_4_ = bf16[29,64,128]{2,1,0:T(8,128)(2,1)S(1)} collective-permute-done((bf16[29,64,128]{2,1,0:T(8,128)(2,1)S(1)}, bf16[29,64,128]{2,1,0:T(8,128)(2,1)S(1)}, u32[]{:S(2)}, u32[]{:S(2)}) %collective-permute-start.17) | collective-permute-done | bytes 475168 | tf_op jit(solution)/shard_map/ppermute | solution.py:32
  136.1 0.6 collective-permute-start.19
  136.8 0.6 collective-permute-start.20
  137.4 2.1 collective-permute-start.21
  139.4 0.6 collective-permute-start.22
  140.0 0.9 collective-permute-start.23
  140.9 4.0 %collective-permute-done.20.refs_6_ = bf16[14,64,128]{2,1,0:T(8,128)(2,1)S(1)} collective-permute-done((bf16[14,64,128]{2,1,0:T(8,128)(2,1)S(1)}, bf16[14,64,128]{2,1,0:T(8,128)(2,1)S(1)}, u32[]{:S(2)}, u32[]{:S(2)}) %collective-permute-start.20) | collective-permute-done | bytes 229408 | tf_op jit(solution)/shard_map/ppermute | solution.py:32
  144.9 0.5 collective-permute-start.24
  145.3 1.5 collective-permute-done.21.refs_7_
  146.9 0.4 collective-permute-done.22.refs_8_
  147.3 2.7 %collective-permute-done.19.refs_5_ = bf16[15,3,64,128]{3,2,1,0:T(8,128)(2,1)S(1)} collective-permute-done((bf16[15,3,64,128]{3,2,1,0:T(8,128)(2,1)S(1)}, bf16[15,3,64,128]{3,2,1,0:T(8,128)(2,1)S(1)}, u32[]{:S(2)}, u32[]{:S(2)}) %collective-permute-start.19) | collective-permute-done | bytes 737312 | tf_op jit(solution)/shard_map/ppermute | solution.py:36
  150.0 2.4 %shard_map.77 = (bf16[29,8,64,128]{3,2,1,0:T(8,128)(2,1)S(1)}, bf16[29,8,64,128]{3,2,1,0:T(8,128)(2,1)}) custom-call(bf16[29,64,128]{2,1,0:T(8,128)(2,1)S(1)} %shard_map.74.refs_0_, bf16[29,64,128]{2,1,0:T(8,128)(2,1)S(1)} %collective-permute-done.14.refs_0_.refs_1_, bf16[29,64,128]{2,1,0:T(8,128)(2,1)S(1)} %collective-permute-done.15.refs_1_.refs_2_, ...), custom_call_target="tpu_custom_call" | custom-call | bytes 11403264 | tf_op jit(solution)/shard_map/pallas_call | solution.py:61
  152.4 11.7 %collective-permute-start.30 = (bf16[29,8,64,128]{3,2,1,0:T(8,128)(2,1)}, bf16[29,8,64,128]{3,2,1,0:T(8,128)(2,1)}, u32[]{:S(2)}, u32[]{:S(2)}) collective-permute-start(bf16[29,8,64,128]{3,2,1,0:T(8,128)(2,1)} %get-tuple-element.84.refs_1_), channel_id=1, source_target_pairs={{0,1},{1,0},{2,3},{3,2},{4,5},{5,4},{6,7},{7,6},{8,9},{9,8},{10,11... | collective-permute-start | bytes 11403272 | tf_op jit(solution)/shard_map/ppermute | solution.py:36
  164.1 6.9 %shard_map.78 = (bf16[64,2,8,464]{3,2,1,0:T(8,128)(2,1)S(1)}, f32[8,128]{1,0:T(8,128)S(1)}) custom-call(s32[8]{0:T(128)S(1)} %stack.35.refs_0_, bf16[29,8,64,128]{3,2,1,0:T(8,128)(2,1)S(1)} %get-tuple-element.76.refs_1_, bf16[464,3712]{1,0:T(8,128)(2,1)S(1)} %copy-done, bf16[464,3712]{1,0:T(8,128)(2,1)} %collective-permute-done.5.refs_4_.refs_3_), custom_call_target="tpu_custom_call" | custom-call | bytes 15597568 | tf_op jit(solution)/shard_map/pallas_call | solution.py:61
  171.0 1.0 copy-done.2
  172.0 2.2 %shard_map.79 = (bf16[29,64,128]{2,1,0:T(8,128)(2,1)}, bf16[29,64,128]{2,1,0:T(8,128)(2,1)}, bf16[29,6,64,128]{3,2,1,0:T(8,128)(2,1)}, f32[8,128]{1,0:T(8,128)S(1)}) custom-call(bf16[29,2,64,128]{3,2,1,0:T(8,128)(2,1)S(1)} %get-tuple-element.78.refs_0_, bf16[29,2,64,128]{3,2,1,0:T(8,128)(2,1)S(1)} %collective-permute-done.23.refs_1_, ...), custom_call_target="tpu_custom_call" | custom-call | bytes 6651904 | tf_op jit(solution)/shard_map/pallas_call | solution.py:61
  174.1 0.6 copy-done.6
  174.7 1.3 collective-permute-start.27
  176.0 0.7 collective-permute-start.25
  176.7 2.0 collective-permute-start.26
  178.7 9.2 %all-to-all-start.1 = ((bf16[64,2,8,464]{3,2,1,0:T(8,128)(2,1)}), bf16[64,2,8,464]{3,2,1,0:T(8,128)(2,1)S(1)}, u32[]{:S(2)}, u32[]{:S(2)}) async-start(bf16[64,2,8,464]{3,2,1,0:T(8,128)(2,1)} %shard_map.80), calls=%async_computation.1 | async-start | bytes 2097152 | tf_op jit(solution)/shard_map/all_to_all | solution.py:155
  188.0 2.0 collective-permute-done.25.refs_2_
  190.0 0.8 collective-permute-start.28
  190.7 0.9 collective-permute-start.29
  191.7 7.0 %shard_map.81 = (f32[464,3712]{1,0:T(8,128)}, f32[8,128]{1,0:T(8,128)S(1)}) custom-call(bf16[464,1024]{1,0:T(8,128)(2,1)S(1)} %get-tuple-element.72.refs_6_.refs_0_, bf16[29,8,64,128]{3,2,1,0:T(8,128)(2,1)} %get-tuple-element.84.refs_1_, bf16[29,8,64,128]{3,2,1,0:T(8,128)(2,1)} %collective-permute-done.30.refs_2_, f32[8,128]{1,0:T(8,128)S(1)} %get-tuple-element.79.refs_3_), custom_call_target="tpu_custom_call" | custom-call | tf_op jit(solution)/shard_map/pallas_call | solution.py:61
  198.7 7.6 %shard_map.82 = (f32[464,3712]{1,0:T(8,128)}, f32[8,128]{1,0:T(8,128)S(1)}) custom-call(bf16[464,1024]{1,0:T(8,128)(2,1)S(1)} %get-tuple-element.73.refs_7_.refs_0_, bf16[29,6,64,128]{3,2,1,0:T(8,128)(2,1)} %get-tuple-element.81.refs_1_, bf16[29,64,128]{2,1,0:T(8,128)(2,1)S(1)} %collective-permute-done.25.refs_2_, ...), custom_call_target="tpu_custom_call" | custom-call | tf_op jit(solution)/shard_map/pallas_call | solution.py:61
  206.6 0.9 shard_map.83
  (34 shorter events, 1.6 us)
Async XLA Ops:
  0.6 45.4 %collective-permute-start = (bf16[464,3712]{1,0:T(8,128)(2,1)}, bf16[464,3712]{1,0:T(8,128)(2,1)}, u32[]{:S(2)}, u32[]{:S(2)}) collective-permute-start(bf16[464,3712]{1,0:T(8,128)(2,1)} %bitcast.11), channel_id=1, source_target_pairs={{0,1},{1,0},{2,3},{3,2},{4,5},{5,4},{6,7},{7,6},{8,9},{9,8},{10,11... | collective-permute-start | bytes 10334216 | tf_op jit(solution)/shard_map/ppermute | solution.py:36
  2.1 53.0 %collective-permute-start.5 = (bf16[464,3712]{1,0:T(8,128)(2,1)}, bf16[464,3712]{1,0:T(8,128)(2,1)}, u32[]{:S(2)}, u32[]{:S(2)}) collective-permute-start(bf16[464,3712]{1,0:T(8,128)(2,1)} %refs_2_.3), channel_id=1, source_target_pairs={{0,1},{1,0},{2,3},{3,2},{4,5},{5,4},{6,7},{7,6},{8,9},{9,8},{10,11... | collective-permute-start | bytes 10334216 | tf_op jit(solution)/shard_map/ppermute | solution.py:36
  2.2 0.9 copy-start.4
  3.1 0.9 copy-start.5
  4.6 1.3 copy-start.1
  5.9 40.1 %all-to-all-start = ((bf16[64,4,8,464]{3,2,1,0:T(8,128)(2,1)}), bf16[64,4,8,464]{3,2,1,0:T(8,128)(2,1)S(1)}, u32[]{:S(2)}, u32[]{:S(2)}) async-start(bf16[64,4,8,464]{3,2,1,0:T(8,128)(2,1)} %copy-done.1), calls=%async_computation | async-start | bytes 4194304 | tf_op jit(solution)/shard_map/all_to_all | solution.py:155
  46.0 9.2 %copy-start = (bf16[464,3712]{1,0:T(8,128)(2,1)S(1)}, bf16[464,3712]{1,0:T(8,128)(2,1)}, u32[]{:S(2)}) copy-start(bf16[464,3712]{1,0:T(8,128)(2,1)} %refs_2_.3) | copy-start | bytes 10334212
  46.0 2.1 %copy-start.3 = (bf16[3712,464]{0,1:T(8,128)(2,1)S(1)}, bf16[3712,464]{0,1:T(8,128)(2,1)}, u32[]{:S(2)}) copy-start(bf16[3712,464]{0,1:T(8,128)(2,1)} %param.7) | copy-start | bytes 10334212
  54.8 33.8 %collective-permute-start.1 = (bf16[24,4,64,128]{3,2,1,0:T(8,128)(2,1)S(1)}, bf16[24,4,64,128]{3,2,1,0:T(8,128)(2,1)S(1)}, u32[]{:S(2)}, u32[]{:S(2)}) collective-permute-start(bf16[24,4,64,128]{3,2,1,0:T(8,128)(2,1)S(1)} %get-tuple-element.47), channel_id=1, source_target_pairs={{0,8},{8,0},{1,9},{9,1},{2,10},{10,2},{3,11},{11,3},{4,12},{12,4},... | collective-permute-start | bytes 4718600 | tf_op jit(solution)/shard_map/ppermute | solution.py:36
  61.8 13.1 %collective-permute-start.8 = (bf16[34,64,128]{2,1,0:T(8,128)(2,1)S(1)}, bf16[34,64,128]{2,1,0:T(8,128)(2,1)S(1)}, u32[]{:S(2)}, u32[]{:S(2)}) collective-permute-start(bf16[34,64,128]{2,1,0:T(8,128)(2,1)S(1)} %get-tuple-element.59), channel_id=1, source_target_pairs={{0,2},{2,4},{4,6},{6,0},{1,3},{3,5},{5,7},{7,1},{8,10},{10,12},{12... | collective-permute-start | bytes 1671176 | tf_op jit(solution)/shard_map/ppermute | solution.py:32
  62.0 12.9 %collective-permute-start.9 = (bf16[34,64,128]{2,1,0:T(8,128)(2,1)S(1)}, bf16[34,64,128]{2,1,0:T(8,128)(2,1)S(1)}, u32[]{:S(2)}, u32[]{:S(2)}) collective-permute-start(bf16[34,64,128]{2,1,0:T(8,128)(2,1)S(1)} %get-tuple-element.60), channel_id=1, source_target_pairs={{0,6},{2,0},{4,2},{6,4},{1,7},{3,1},{5,3},{7,5},{8,14},{10,8},{12,... | collective-permute-start | bytes 1671176 | tf_op jit(solution)/shard_map/ppermute | solution.py:32
  64.6 27.5 %collective-permute-start.6 = (bf16[34,64,128]{2,1,0:T(8,128)(2,1)S(1)}, bf16[34,64,128]{2,1,0:T(8,128)(2,1)S(1)}, u32[]{:S(2)}, u32[]{:S(2)}) collective-permute-start(bf16[34,64,128]{2,1,0:T(8,128)(2,1)S(1)} %get-tuple-element.55), channel_id=1, source_target_pairs={{0,6},{2,0},{4,2},{6,4},{1,7},{3,1},{5,3},{7,5},{8,14},{10,8},{12,... | collective-permute-start | bytes 1671176 | tf_op jit(solution)/shard_map/ppermute | solution.py:32
  64.6 27.5 %collective-permute-start.7 = (bf16[34,64,128]{2,1,0:T(8,128)(2,1)S(1)}, bf16[34,64,128]{2,1,0:T(8,128)(2,1)S(1)}, u32[]{:S(2)}, u32[]{:S(2)}) collective-permute-start(bf16[34,64,128]{2,1,0:T(8,128)(2,1)S(1)} %get-tuple-element.56), channel_id=1, source_target_pairs={{0,2},{2,4},{4,6},{6,0},{1,3},{3,5},{5,7},{7,1},{8,10},{10,12},{12... | collective-permute-start | bytes 1671176 | tf_op jit(solution)/shard_map/ppermute | solution.py:32
  75.4 23.4 %collective-permute-start.10 = (bf16[34,64,128]{2,1,0:T(8,128)(2,1)S(1)}, bf16[34,64,128]{2,1,0:T(8,128)(2,1)S(1)}, u32[]{:S(2)}, u32[]{:S(2)}) collective-permute-start(bf16[34,64,128]{2,1,0:T(8,128)(2,1)S(1)} %get-tuple-element.63), channel_id=1, source_target_pairs={{0,2},{2,4},{4,6},{6,0},{1,3},{3,5},{5,7},{7,1},{8,10},{10,12},{12... | collective-permute-start | bytes 1671176 | tf_op jit(solution)/shard_map/ppermute | solution.py:32
  75.7 23.1 %collective-permute-start.11 = (bf16[34,64,128]{2,1,0:T(8,128)(2,1)S(1)}, bf16[34,64,128]{2,1,0:T(8,128)(2,1)S(1)}, u32[]{:S(2)}, u32[]{:S(2)}) collective-permute-start(bf16[34,64,128]{2,1,0:T(8,128)(2,1)S(1)} %get-tuple-element.64), channel_id=1, source_target_pairs={{0,6},{2,0},{4,2},{6,4},{1,7},{3,1},{5,3},{7,5},{8,14},{10,8},{12,... | collective-permute-start | bytes 1671176 | tf_op jit(solution)/shard_map/ppermute | solution.py:32
  88.6 22.4 %collective-permute-start.13 = (bf16[512,1024]{1,0:T(8,128)(2,1)S(1)}, bf16[512,1024]{1,0:T(8,128)(2,1)S(1)}, u32[]{:S(2)}, u32[]{:S(2)}) collective-permute-start(bf16[512,1024]{1,0:T(8,128)(2,1)S(1)} %get-tuple-element.68), channel_id=1, source_target_pairs={{0,1},{1,0},{2,3},{3,2},{4,5},{5,4},{6,7},{7,6},{8,9},{9,8},{10,11... | collective-permute-start | bytes 3145736 | tf_op jit(solution)/shard_map/ppermute | solution.py:36
  99.3 11.0 %collective-permute-start.12 = (bf16[34,64,128]{2,1,0:T(8,128)(2,1)S(1)}, bf16[34,64,128]{2,1,0:T(8,128)(2,1)S(1)}, u32[]{:S(2)}, u32[]{:S(2)}) collective-permute-start(bf16[34,64,128]{2,1,0:T(8,128)(2,1)S(1)} %get-tuple-element.66), channel_id=1, source_target_pairs={{0,8},{8,0},{1,9},{9,1},{2,10},{10,2},{3,11},{11,3},{4,12},{12,4},... | collective-permute-start | bytes 1671176 | tf_op jit(solution)/shard_map/ppermute | solution.py:36
  100.5 8.2 %collective-permute-start.2 = (bf16[24,64,128]{2,1,0:T(8,128)(2,1)S(1)}, bf16[24,64,128]{2,1,0:T(8,128)(2,1)S(1)}, u32[]{:S(2)}, u32[]{:S(2)}) collective-permute-start(bf16[24,64,128]{2,1,0:T(8,128)(2,1)S(1)} %get-tuple-element.49), channel_id=1, source_target_pairs={{0,2},{2,4},{4,6},{6,0},{1,3},{3,5},{5,7},{7,1},{8,10},{10,12},{12... | collective-permute-start | bytes 1179656 | tf_op jit(solution)/shard_map/ppermute | solution.py:32
  100.8 10.2 %collective-permute-start.3 = (bf16[24,64,128]{2,1,0:T(8,128)(2,1)S(1)}, bf16[24,64,128]{2,1,0:T(8,128)(2,1)S(1)}, u32[]{:S(2)}, u32[]{:S(2)}) collective-permute-start(bf16[24,64,128]{2,1,0:T(8,128)(2,1)S(1)} %get-tuple-element.50), channel_id=1, source_target_pairs={{0,6},{2,0},{4,2},{6,4},{1,7},{3,1},{5,3},{7,5},{8,14},{10,8},{12,... | collective-permute-start | bytes 1179656 | tf_op jit(solution)/shard_map/ppermute | solution.py:32
  103.2 14.3 %collective-permute-start.4 = (bf16[24,64,128]{2,1,0:T(8,128)(2,1)S(1)}, bf16[24,64,128]{2,1,0:T(8,128)(2,1)S(1)}, u32[]{:S(2)}, u32[]{:S(2)}) collective-permute-start(bf16[24,64,128]{2,1,0:T(8,128)(2,1)S(1)} %get-tuple-element.51), channel_id=1, source_target_pairs={{0,4},{2,6},{4,0},{6,2},{1,5},{3,7},{5,1},{7,3},{8,12},{10,14},{12... | collective-permute-start | bytes 1179656 | tf_op jit(solution)/shard_map/ppermute | solution.py:32
  117.8 7.6 %collective-permute-start.14 = (bf16[29,64,128]{2,1,0:T(8,128)(2,1)S(1)}, bf16[29,64,128]{2,1,0:T(8,128)(2,1)S(1)}, u32[]{:S(2)}, u32[]{:S(2)}) collective-permute-start(bf16[29,64,128]{2,1,0:T(8,128)(2,1)S(1)} %shard_map.74.refs_0_), channel_id=1, source_target_pairs={{0,8},{8,0},{1,9},{9,1},{2,10},{10,2},{3,11},{11,3},{4,12},{12,4},... | collective-permute-start | bytes 1425416 | tf_op jit(solution)/shard_map/ppermute | solution.py:36
  118.4 10.3 %collective-permute-start.15 = (bf16[29,64,128]{2,1,0:T(8,128)(2,1)S(1)}, bf16[29,64,128]{2,1,0:T(8,128)(2,1)S(1)}, u32[]{:S(2)}, u32[]{:S(2)}) collective-permute-start(bf16[29,64,128]{2,1,0:T(8,128)(2,1)S(1)} %shard_map.74.refs_0_), channel_id=1, source_target_pairs={{0,2},{2,4},{4,6},{6,0},{1,3},{3,5},{5,7},{7,1},{8,10},{10,12},{12... | collective-permute-start | bytes 1425416 | tf_op jit(solution)/shard_map/ppermute | solution.py:32
  119.0 10.5 %collective-permute-start.16 = (bf16[29,64,128]{2,1,0:T(8,128)(2,1)S(1)}, bf16[29,64,128]{2,1,0:T(8,128)(2,1)S(1)}, u32[]{:S(2)}, u32[]{:S(2)}) collective-permute-start(bf16[29,64,128]{2,1,0:T(8,128)(2,1)S(1)} %shard_map.74.refs_0_), channel_id=1, source_target_pairs={{0,6},{2,0},{4,2},{6,4},{1,7},{3,1},{5,3},{7,5},{8,14},{10,8},{12,... | collective-permute-start | bytes 1425416 | tf_op jit(solution)/shard_map/ppermute | solution.py:32
  121.1 14.9 %collective-permute-start.17 = (bf16[29,64,128]{2,1,0:T(8,128)(2,1)S(1)}, bf16[29,64,128]{2,1,0:T(8,128)(2,1)S(1)}, u32[]{:S(2)}, u32[]{:S(2)}) collective-permute-start(bf16[29,64,128]{2,1,0:T(8,128)(2,1)S(1)} %shard_map.74.refs_0_), channel_id=1, source_target_pairs={{0,4},{2,6},{4,0},{6,2},{1,5},{3,7},{5,1},{7,3},{8,12},{10,14},{12... | collective-permute-start | bytes 1425416 | tf_op jit(solution)/shard_map/ppermute | solution.py:32
  121.1 14.9 %collective-permute-start.18 = (bf16[29,64,128]{2,1,0:T(8,128)(2,1)S(1)}, bf16[29,64,128]{2,1,0:T(8,128)(2,1)S(1)}, u32[]{:S(2)}, u32[]{:S(2)}) collective-permute-start(bf16[29,64,128]{2,1,0:T(8,128)(2,1)S(1)} %get-tuple-element.69.refs_4_), channel_id=1, source_target_pairs={{0,8},{8,0},{1,9},{9,1},{2,10},{10,2},{3,11},{11,3},{4,12},{12,4},... | collective-permute-start | bytes 1425416 | tf_op jit(solution)/shard_map/ppermute | solution.py:36
  136.1 13.9 %collective-permute-start.19 = (bf16[15,3,64,128]{3,2,1,0:T(8,128)(2,1)S(1)}, bf16[15,3,64,128]{3,2,1,0:T(8,128)(2,1)S(1)}, u32[]{:S(2)}, u32[]{:S(2)}) collective-permute-start(bf16[15,3,64,128]{3,2,1,0:T(8,128)(2,1)S(1)} %get-tuple-element.74), channel_id=1, source_target_pairs={{0,8},{8,0},{1,9},{9,1},{2,10},{10,2},{3,11},{11,3},{4,12},{12,4},... | collective-permute-start | bytes 2211848 | tf_op jit(solution)/shard_map/ppermute | solution.py:36
  136.8 8.1 %collective-permute-start.20 = (bf16[14,64,128]{2,1,0:T(8,128)(2,1)S(1)}, bf16[14,64,128]{2,1,0:T(8,128)(2,1)S(1)}, u32[]{:S(2)}, u32[]{:S(2)}) collective-permute-start(bf16[14,64,128]{2,1,0:T(8,128)(2,1)S(1)} %get-tuple-element.75), channel_id=1, source_target_pairs={{0,2},{2,4},{4,6},{6,0},{1,3},{3,5},{5,7},{7,1},{8,10},{10,12},{12... | collective-permute-start | bytes 688136 | tf_op jit(solution)/shard_map/ppermute | solution.py:32
  137.4 9.5 %collective-permute-start.21 = (bf16[14,64,128]{2,1,0:T(8,128)(2,1)S(1)}, bf16[14,64,128]{2,1,0:T(8,128)(2,1)S(1)}, u32[]{:S(2)}, u32[]{:S(2)}) collective-permute-start(bf16[14,64,128]{2,1,0:T(8,128)(2,1)S(1)} %get-tuple-element.75), channel_id=1, source_target_pairs={{0,6},{2,0},{4,2},{6,4},{1,7},{3,1},{5,3},{7,5},{8,14},{10,8},{12,... | collective-permute-start | bytes 688136 | tf_op jit(solution)/shard_map/ppermute | solution.py:32
  139.4 7.9 %collective-permute-start.22 = (bf16[14,64,128]{2,1,0:T(8,128)(2,1)S(1)}, bf16[14,64,128]{2,1,0:T(8,128)(2,1)S(1)}, u32[]{:S(2)}, u32[]{:S(2)}) collective-permute-start(bf16[14,64,128]{2,1,0:T(8,128)(2,1)S(1)} %get-tuple-element.75), channel_id=1, source_target_pairs={{0,4},{2,6},{4,0},{6,2},{1,5},{3,7},{5,1},{7,3},{8,12},{10,14},{12... | collective-permute-start | bytes 688136 | tf_op jit(solution)/shard_map/ppermute | solution.py:32
  140.0 32.0 %collective-permute-start.23 = (bf16[29,2,64,128]{3,2,1,0:T(8,128)(2,1)S(1)}, bf16[29,2,64,128]{3,2,1,0:T(8,128)(2,1)S(1)}, u32[]{:S(2)}, u32[]{:S(2)}) collective-permute-start(bf16[29,2,64,128]{3,2,1,0:T(8,128)(2,1)S(1)} %get-tuple-element.78.refs_0_), channel_id=1, source_target_pairs={{0,2},{2,4},{4,6},{6,0},{1,3},{3,5},{5,7},{7,1},{8,10},{10,12},{12... | collective-permute-start | bytes 2850824 | tf_op jit(solution)/shard_map/ppermute | solution.py:32
  144.9 27.1 %collective-permute-start.24 = (bf16[29,2,64,128]{3,2,1,0:T(8,128)(2,1)S(1)}, bf16[29,2,64,128]{3,2,1,0:T(8,128)(2,1)S(1)}, u32[]{:S(2)}, u32[]{:S(2)}) collective-permute-start(bf16[29,2,64,128]{3,2,1,0:T(8,128)(2,1)S(1)} %get-tuple-element.78.refs_0_), channel_id=1, source_target_pairs={{0,6},{2,0},{4,2},{6,4},{1,7},{3,1},{5,3},{7,5},{8,14},{10,8},{12,... | collective-permute-start | bytes 2850824 | tf_op jit(solution)/shard_map/ppermute | solution.py:32
  152.4 39.3 %collective-permute-start.30 = (bf16[29,8,64,128]{3,2,1,0:T(8,128)(2,1)}, bf16[29,8,64,128]{3,2,1,0:T(8,128)(2,1)}, u32[]{:S(2)}, u32[]{:S(2)}) collective-permute-start(bf16[29,8,64,128]{3,2,1,0:T(8,128)(2,1)} %get-tuple-element.84.refs_1_), channel_id=1, source_target_pairs={{0,1},{1,0},{2,3},{3,2},{4,5},{5,4},{6,7},{7,6},{8,9},{9,8},{10,11... | collective-permute-start | bytes 11403272 | tf_op jit(solution)/shard_map/ppermute | solution.py:36
  171.0 1.0 copy-start.2
  174.1 0.6 copy-start.6
  174.7 24.0 %collective-permute-start.27 = (bf16[29,6,64,128]{3,2,1,0:T(8,128)(2,1)}, bf16[29,6,64,128]{3,2,1,0:T(8,128)(2,1)}, u32[]{:S(2)}, u32[]{:S(2)}) collective-permute-start(bf16[29,6,64,128]{3,2,1,0:T(8,128)(2,1)} %get-tuple-element.81.refs_1_), channel_id=1, source_target_pairs={{0,1},{1,0},{2,3},{3,2},{4,5},{5,4},{6,7},{7,6},{8,9},{9,8},{10,11... | collective-permute-start | bytes 8552456 | tf_op jit(solution)/shard_map/ppermute | solution.py:36
  176.0 13.9 %collective-permute-start.25 = (bf16[29,64,128]{2,1,0:T(8,128)(2,1)}, bf16[29,64,128]{2,1,0:T(8,128)(2,1)S(1)}, u32[]{:S(2)}, u32[]{:S(2)}) collective-permute-start(bf16[29,64,128]{2,1,0:T(8,128)(2,1)} %get-tuple-element.82), channel_id=1, source_target_pairs={{0,2},{2,4},{4,6},{6,0},{1,3},{3,5},{5,7},{7,1},{8,10},{10,12},{12... | collective-permute-start | bytes 1425416 | tf_op jit(solution)/shard_map/ppermute | solution.py:32
  176.7 14.0 %collective-permute-start.26 = (bf16[29,64,128]{2,1,0:T(8,128)(2,1)}, bf16[29,64,128]{2,1,0:T(8,128)(2,1)}, u32[]{:S(2)}, u32[]{:S(2)}) collective-permute-start(bf16[29,64,128]{2,1,0:T(8,128)(2,1)} %get-tuple-element.83), channel_id=1, source_target_pairs={{0,6},{2,0},{4,2},{6,4},{1,7},{3,1},{5,3},{7,5},{8,14},{10,8},{12,... | collective-permute-start | bytes 1425416 | tf_op jit(solution)/shard_map/ppermute | solution.py:32
  178.7 27.9 %all-to-all-start.1 = ((bf16[64,2,8,464]{3,2,1,0:T(8,128)(2,1)}), bf16[64,2,8,464]{3,2,1,0:T(8,128)(2,1)S(1)}, u32[]{:S(2)}, u32[]{:S(2)}) async-start(bf16[64,2,8,464]{3,2,1,0:T(8,128)(2,1)} %shard_map.80), calls=%async_computation.1 | async-start | bytes 2097152 | tf_op jit(solution)/shard_map/all_to_all | solution.py:155
  190.0 8.7 %collective-permute-start.28 = (bf16[29,64,128]{2,1,0:T(8,128)(2,1)S(1)}, bf16[29,64,128]{2,1,0:T(8,128)(2,1)S(1)}, u32[]{:S(2)}, u32[]{:S(2)}) collective-permute-start(bf16[29,64,128]{2,1,0:T(8,128)(2,1)S(1)} %collective-permute-done.25.refs_2_), channel_id=1, source_target_pairs={{0,1},{1,0},{2,3},{3,2},{4,5},{5,4},{6,7},{7,6},{8,9},{9,8},{10,11... | collective-permute-start | bytes 1425416 | tf_op jit(solution)/shard_map/ppermute | solution.py:36
  190.7 8.0 %collective-permute-start.29 = (bf16[29,64,128]{2,1,0:T(8,128)(2,1)}, bf16[29,64,128]{2,1,0:T(8,128)(2,1)S(1)}, u32[]{:S(2)}, u32[]{:S(2)}) collective-permute-start(bf16[29,64,128]{2,1,0:T(8,128)(2,1)} %collective-permute-done.26.refs_3_), channel_id=1, source_target_pairs={{0,1},{1,0},{2,3},{3,2},{4,5},{5,4},{6,7},{7,6},{8,9},{9,8},{10,11... | collective-permute-start | bytes 1425416 | tf_op jit(solution)/shard_map/ppermute | solution.py:36
